TPU v7x, 512 devices: a whole 4x4x16 slice. The times are simulated.
512 devices in a mesh: seq: 32 (over z, core), item: 16 (over y, x).
Axes of the slice: x: 4, y: 4, z: 16, core: 2. Of those that a mesh axis runs over, the one named last changes fastest.
Arguments:
- history: bfloat16 [16, 4096, 512], P('item', 'seq'), may hold values from -6 to 6
- w_in: bfloat16 [512, 1536], replicated, may hold values from -0.25 to 0.25
- w_out: bfloat16 [512, 512], replicated, may hold values from -0.25 to 0.25
- item_table: bfloat16 [65536, 512], P(('seq', 'item')), may hold values from -6 to 6
- w_item_in: bfloat16 [512, 1024], replicated, may hold values from -0.25 to 0.25
- w_item_out: bfloat16 [1024, 512], replicated, may hold values from -0.1875 to 0.1875
- req_rows: int32 [16, 32, 512, 2], P('item', 'seq'), may hold values from 0 to 127
- req_counts: int32 [16, 32, 512], P('item', 'seq'), may hold values from 1 to 2, as said below
- labels: int32 [16, 4096, 4], P('item', 'seq'), may hold values from -1 to 1023, as said below
Outputs:
- position_loss: float32 [16, 4096], P('item', 'seq')
- item_table_gradient: float32 [65536, 512], P(('seq', 'item'))
Inputs may be any that keep to these rules, and one draw needn't show every extreme that they name: `req_rows`: slots at or beyond the block's count toward that owner are padding. `req_counts`: every history block uses all 2 slots toward some owner, and in every draw some owner is asked for 2 rows by every block. `labels`: A slot named is a used slot of the position's block; -1 names none; a slot may be named twice.
All inputs are finite; a program needn't handle non-finite values.
Results may differ from a plain program's by a relative error of at most 0.0085.
Values may be sent and summed in bfloat16 or wider, within the bound.
No kernel may reach another device: no remote copies, remote signals or barrier semaphores. Data moves between devices by JAX's collectives and lax.ppermute only.
A program may use at most 64 MiB of HBM per device.

v0:
```python
import jax
import jax.numpy as jnp
from jax import lax
from jax.sharding import PartitionSpec as P

HEADS = 4
DQK = 64


sharpness_divisor = 0.02
norm_eps = 1e-05
unit_eps = 1e-06


def silu_slope(inputs):
    sigma = jax.nn.sigmoid(inputs)
    return sigma * (1.0 + inputs * (1.0 - sigma))


def split_product(left, weight):
    contract = (((1,), (1,)), ((), ()))
    high = left.astype(jnp.bfloat16)
    low = (left - high.astype(jnp.float32)).astype(jnp.bfloat16)
    first = lax.dot_general(high, weight, contract, preferred_element_type=jnp.float32)
    return first + lax.dot_general(low, weight, contract, preferred_element_type=jnp.float32)


def item_forward(table_rows, w_item_in, w_item_out):
    hidden_in = jnp.dot(table_rows, w_item_in, preferred_element_type=jnp.float32)
    hidden = jax.nn.silu(hidden_in).astype(jnp.bfloat16)
    raw_embed = jnp.dot(hidden, w_item_out, preferred_element_type=jnp.float32)
    inv_norm = lax.rsqrt(jnp.sum(raw_embed * raw_embed, axis=-1, keepdims=True) + unit_eps)
    embedding = (raw_embed * inv_norm).astype(jnp.bfloat16)
    return (hidden_in, raw_embed, inv_norm, embedding)


def item_backward(hidden_in, raw_embed, inv_norm, vector_derivative_matrix, w_item_in, w_item_out):
    unit = raw_embed * inv_norm
    raw_grad = (
        vector_derivative_matrix
        - unit * jnp.sum(unit * vector_derivative_matrix, axis=-1, keepdims=True)
    ) * inv_norm
    hidden_grad = split_product(raw_grad, w_item_out)
    input_grad = hidden_grad * silu_slope(hidden_in)
    return split_product(input_grad, w_item_in)


def block_loss(customer_vector_entries, catalog_entries, counts, label_slots):
    slot_total = catalog_entries.shape[0]
    capacity = slot_total // counts.shape[0]
    similarity_matrix = (
        lax.dot_general(
            customer_vector_entries,
            catalog_entries,
            (((1,), (1,)), ((), ())),
            preferred_element_type=jnp.float32,
        )
        / sharpness_divisor
    )
    used = (jnp.arange(capacity, dtype=jnp.int32)[None, :] < counts[:, None]).reshape(-1)
    exponent = jnp.where(used[None, :], jnp.exp(similarity_matrix), 0.0)
    total = jnp.sum(exponent, axis=-1)
    log_total = jnp.log(total)
    slot_ids = jnp.arange(slot_total, dtype=jnp.int32)
    positive_hits = jnp.zeros(similarity_matrix.shape, jnp.float32)
    for column in range(label_slots.shape[1]):
        positive_hits = positive_hits + (
            label_slots[:, column][:, None] == slot_ids[None, :]
        ).astype(jnp.float32)
    positives = jnp.sum((label_slots >= 0).astype(jnp.float32), axis=-1)
    divisor = jnp.maximum(positives, 1.0)
    position_loss = (
        jnp.sum(positive_hits * (log_total[:, None] - similarity_matrix), axis=-1) / divisor
    )
    probability = exponent / total[:, None]
    similarity_derivative = (
        (positives / divisor)[:, None] * probability - positive_hits / divisor[:, None]
    ).astype(jnp.bfloat16)
    vector_derivative_matrix = (
        lax.dot_general(
            similarity_derivative,
            customer_vector_entries,
            (((0,), (0,)), ((), ())),
            preferred_element_type=jnp.float32,
        )
        / sharpness_divisor
    )
    return (position_loss, vector_derivative_matrix)


def on_device(
    history, w_in, w_out, item_table, w_item_in, w_item_out, req_rows, req_counts, labels
):
    seq_count = lax.axis_size("seq")
    item_count = lax.axis_size("item")
    history_rows = history[0]
    token_count = history_rows.shape[0]
    model_width = history_rows.shape[1]
    query_width = HEADS * DQK
    head_value = model_width // HEADS
    first_position = lax.axis_index("seq") * token_count
    projected = jnp.dot(history_rows, w_in, preferred_element_type=jnp.float32)
    activated = jax.nn.silu(projected)
    gate_units = activated[:, :model_width]
    value_rows = activated[:, model_width : 2 * model_width].astype(jnp.bfloat16)
    query_rows = activated[:, 2 * model_width : 2 * model_width + query_width].astype(jnp.bfloat16)
    key_rows = activated[:, 2 * model_width + query_width :].astype(jnp.bfloat16)
    query_heads = query_rows.reshape(token_count, HEADS, DQK)
    positions = first_position + jnp.arange(token_count, dtype=jnp.int32)
    key_piece = lax.all_gather(key_rows, "seq", axis=0, tiled=True)
    value_piece = lax.all_gather(value_rows, "seq", axis=0, tiled=True)
    key_count = key_piece.shape[0]
    key_heads = key_piece.reshape(key_count, HEADS, DQK)
    value_heads = value_piece.reshape(key_count, HEADS, head_value)
    similarity_matrix = jnp.einsum(
        "qhd,khd->hqk", query_heads, key_heads, preferred_element_type=jnp.float32
    ) * DQK ** (-0.5)
    key_positions = jnp.arange(key_count, dtype=jnp.int32)
    allowed = key_positions[None, None, :] <= positions[None, :, None]
    weights = jnp.where(allowed, jax.nn.silu(similarity_matrix), 0.0).astype(jnp.bfloat16)
    attended = jnp.einsum("hqk,khd->qhd", weights, value_heads, preferred_element_type=jnp.float32)
    attended = attended.reshape(token_count, model_width)
    row_mean = jnp.mean(attended, axis=-1, keepdims=True)
    centered = attended - row_mean
    variance = jnp.mean(centered * centered, axis=-1, keepdims=True)
    normed = centered * lax.rsqrt(variance + norm_eps)
    mixed_rows = (normed * gate_units).astype(jnp.bfloat16)
    updated = history_rows.astype(jnp.float32) + jnp.dot(
        mixed_rows, w_out, preferred_element_type=jnp.float32
    )
    scale = lax.rsqrt(jnp.sum(updated * updated, axis=-1, keepdims=True) + unit_eps)
    customer_vector_entries = (updated * scale).astype(jnp.bfloat16)
    wanted = req_rows[0, 0]
    counts = req_counts[0, 0]
    capacity = wanted.shape[1]
    slot_total = seq_count * item_count * capacity
    asked_rows = lax.all_to_all(
        lax.all_to_all(
            wanted.reshape(seq_count, item_count, capacity),
            "seq",
            split_axis=0,
            concat_axis=0,
            tiled=True,
        ),
        "item",
        split_axis=1,
        concat_axis=1,
        tiled=True,
    )
    asked_flat = asked_rows.reshape(slot_total)
    answer = jnp.take(item_table, asked_flat, axis=0)
    answer = answer.reshape(seq_count, item_count, capacity, answer.shape[1])
    arrived = lax.all_to_all(
        lax.all_to_all(answer, "seq", split_axis=0, concat_axis=0, tiled=True),
        "item",
        split_axis=1,
        concat_axis=1,
        tiled=True,
    )
    arrived = arrived.reshape(slot_total, arrived.shape[3])
    hidden_in, raw_embed, inv_norm, catalog_entries = item_forward(arrived, w_item_in, w_item_out)
    position_loss, vector_derivative_matrix = block_loss(
        customer_vector_entries, catalog_entries, counts, labels[0]
    )
    outgoing = item_backward(
        hidden_in, raw_embed, inv_norm, vector_derivative_matrix, w_item_in, w_item_out
    )
    outgoing = outgoing.reshape(seq_count, item_count, capacity, outgoing.shape[1])
    returned = lax.all_to_all(
        lax.all_to_all(outgoing, "seq", split_axis=0, concat_axis=0, tiled=True),
        "item",
        split_axis=1,
        concat_axis=1,
        tiled=True,
    )
    returned = returned.reshape(slot_total, returned.shape[3])
    row_count = item_table.shape[0]
    onehot = (jnp.arange(row_count, dtype=jnp.int32)[:, None] == asked_flat[None, :]).astype(
        jnp.float32
    )
    summed = jnp.dot(onehot, returned, precision=lax.Precision.HIGHEST)
    return (position_loss[None, :], summed)


def solution(mesh):
    placed = (
        P("item", "seq", None),
        P(),
        P(),
        P(("seq", "item"), None),
        P(),
        P(),
        P("item", "seq", None, None),
        P("item", "seq", None),
        P("item", "seq", None),
    )
    return jax.shard_map(
        on_device,
        mesh=mesh,
        in_specs=placed,
        out_specs=(P("item", "seq"), P(("seq", "item"), None)),
        check_vma=False,
    )
```

profile of v0, /device:TPU:1, one launch (start us, length us, event | category | flops | bytes accessed | tf_op | source)
XLA Modules:
  0.0 373.2 jit_solution(2176385896085240551)
XLA Ops:
  12.4 28.7 %all_to_all.30 = s32[32,16,2]{1,2,0:T(2,128)S(1)} all-to-all(s32[32,16,2]{1,2,0:T(2,128)S(1)} %copy.51), channel_id=1, replica_groups=mesh['seq'=32,'item'=16] {'seq'}, dimensions={0} | all-to-all | bytes 8192 | tf_op jit(solution)/shard_map/all_to_all | solution.py:138
  41.1 13.0 %all_to_all.31 = s32[32,16,2]{0,2,1:T(2,128)S(1)} all-to-all(s32[32,16,2]{0,2,1:T(2,128)S(1)} %copy.52), channel_id=1, replica_groups=mesh['seq'=32,'item'=16] {'item'}, dimensions={1} | all-to-all | bytes 8192 | tf_op jit(solution)/shard_map/all_to_all | solution.py:137
  54.5 4.0 %gather_fusion = bf16[1024,512]{1,0:T(8,128)(2,1)S(1)} fusion(bf16[128,512]{1,0:T(8,128)(2,1)S(1)} %copy-done.1, s32[1024]{0:T(1024)S(1)} %broadcast_clamp_fusion), kind=kCustom, calls=%fused_computation | custom fusion | bytes 2101248 | tf_op jit(solution)/shard_map/jit(_take)/gather | solution.py:151
  60.0 3.1 broadcast_select_fusion
  63.1 6.1 %all-to-all-start.2 = ((bf16[32,16,2,512]{3,2,1,0:T(2,128)(2,1)}), bf16[32,16,2,512]{3,2,1,0:T(2,128)(2,1)S(1)}, u32[]{:S(2)}, u32[]{:S(2)}) async-start(bf16[32,16,2,512]{3,2,1,0:T(2,128)(2,1)} %broadcast_select_fusion), calls=%async_computation.2 | async-start | bytes 2097152 | tf_op jit(solution)/shard_map/all_to_all | solution.py:154
  69.7 55.1 %all-to-all-done.2 = bf16[32,16,2,512]{3,2,1,0:T(2,128)(2,1)S(1)} async-done(((bf16[32,16,2,512]{3,2,1,0:T(2,128)(2,1)}), bf16[32,16,2,512]{3,2,1,0:T(2,128)(2,1)S(1)}, u32[]{:S(2)}, u32[]{:S(2)}) %all-to-all-start.2) | async-done | bytes 1048608 | tf_op jit(solution)/shard_map/all_to_all | solution.py:154
  126.9 3.9 %all-to-all-start.3 = ((bf16[32,16,2,512]{3,2,0,1:T(2,128)(2,1)}), bf16[32,16,2,512]{3,2,0,1:T(2,128)(2,1)S(1)}, u32[]{:S(2)}, u32[]{:S(2)}) async-start(bf16[32,16,2,512]{3,2,0,1:T(2,128)(2,1)} %copy.55), calls=%async_computation.3 | async-start | bytes 2097152 | tf_op jit(solution)/shard_map/all_to_all | solution.py:153
  132.0 4.1 %copy.48 = bf16[4096,256]{0,1:T(8,128)(2,1)} copy(bf16[4096,256]{1,0:T(8,128)(2,1)} %all-gather.5.cloned.1.call-done) | data formatting | bytes 4194304 | tf_op jit(solution)/shard_map/all_gather | solution.py:110
  136.1 11.0 %all-to-all-done.3 = bf16[32,16,2,512]{3,2,0,1:T(2,128)(2,1)S(1)} async-done(((bf16[32,16,2,512]{3,2,0,1:T(2,128)(2,1)}), bf16[32,16,2,512]{3,2,0,1:T(2,128)(2,1)S(1)}, u32[]{:S(2)}, u32[]{:S(2)}) %all-to-all-start.3) | async-done | bytes 1048608 | tf_op jit(solution)/shard_map/all_to_all | solution.py:153
  151.5 2.6 fusion.45
  154.1 2.7 multiply_reduce_fusion.1
  156.9 18.3 %all-gather.3.cloned.1.call-done = bf16[4096,512]{1,0:T(8,128)(2,1)} async-done(((bf16[128,512]{1,0:T(8,128)(2,1)}), bf16[4096,512]{1,0:T(8,128)(2,1)}) %all-gather.3.cloned.1.call-update) | async-done | bytes 4194320 | tf_op jit(solution)/shard_map/all_gather | solution.py:111
  175.1 6.4 %copy.60 = bf16[4096,512]{0,1:T(8,128)(2,1)} copy(bf16[4096,512]{1,0:T(8,128)(2,1)} %all-gather.3.cloned.1.call-done) | data formatting | bytes 8388608 | tf_op jit(solution)/shard_map/reshape | solution.py:114
  181.5 6.7 %fusion.44 = (f32[128]{0:T(128)S(1)}, f32[4,128,128]{2,1,0:T(8,128)S(1)}) fusion(bf16[4096,4,128]{0,2,1:T(8,128)(2,1)} %bitcast.48, bf16[128,4,64]{0,2,1:T(8,128)(2,1)S(1)} %bitcast.51, bf16[4096,4,64]{0,2,1:T(8,128)(2,1)} %bitcast.49, pred[128,4096]{1,0:T(8,128)(4,1)} %iota_compare_fusion), kind=kOutput, calls=%fused_computation.87 | convolution fusion | flops 820051840 | bytes 7143936 | tf_op jit(solution)/shard_map/hqk,khd->qhd/dot_general | solution.py:121
  196.7 2.5 multiply_multiply_fusion
  200.5 2.7 fusion.2
  203.1 3.5 reshape.177
  206.6 108.3 %all_to_all.32 = f32[32,16,2,512]{3,2,1,0:T(2,128)S(1)} all-to-all(f32[32,16,2,512]{3,2,1,0:T(2,128)} %reshape.177), channel_id=1, replica_groups=mesh['seq'=32,'item'=16] {'seq'}, dimensions={0} | all-to-all | bytes 4194304 | tf_op jit(solution)/shard_map/all_to_all | solution.py:170
  314.8 2.4 copy.58
  317.2 6.7 %all-to-all-start.5 = ((f32[32,16,2,512]{3,2,0,1:T(2,128)}), f32[32,16,2,512]{3,2,0,1:T(2,128)}, u32[]{:S(2)}, u32[]{:S(2)}) async-start(f32[32,16,2,512]{3,2,0,1:T(2,128)} %copy.58), calls=%async_computation.5 | async-start | bytes 4194304 | tf_op jit(solution)/shard_map/all_to_all | solution.py:169
  324.2 31.2 %all-to-all-done.5 = f32[32,16,2,512]{3,2,0,1:T(2,128)} async-done(((f32[32,16,2,512]{3,2,0,1:T(2,128)}), f32[32,16,2,512]{3,2,0,1:T(2,128)}, u32[]{:S(2)}, u32[]{:S(2)}) %all-to-all-start.5) | async-done | bytes 2097184 | tf_op jit(solution)/shard_map/all_to_all | solution.py:169
  355.4 4.1 %copy.59 = f32[32,16,2,512]{3,2,1,0:T(2,128)} copy(f32[32,16,2,512]{3,2,0,1:T(2,128)} %all-to-all-done.5) | data formatting | bytes 4194304 | tf_op jit(solution)/shard_map/all_to_all | solution.py:169
  359.5 3.7 reshape.178
  363.2 3.2 fusion.11
  (65 shorter events, 25.0 us)
Async XLA Ops:
  7.2 1.4 copy-start
  7.2 5.1 %copy-start.7 = (s32[1,1,512,2]{2,3,1,0:T(2,128)S(1)}, s32[1,1,512,2]{2,3,1,0:T(2,128)}, u32[]{:S(2)}) copy-start(s32[1,1,512,2]{2,3,1,0:T(2,128)} %param.15) | copy-start | bytes 12292
  7.2 47.3 %copy-start.1 = (bf16[128,512]{1,0:T(8,128)(2,1)S(1)}, bf16[128,512]{1,0:T(8,128)(2,1)}, u32[]{:S(2)}) copy-start(bf16[128,512]{1,0:T(8,128)(2,1)} %param.12) | copy-start | bytes 393220
  7.2 124.8 %all-gather.5.cloned.1.call-start = ((), (), s32[]{:S(2)}) async-start(), calls=%async_computation.7 | async-start | bytes 2162688 | tf_op jit(solution)/shard_map/all_gather | solution.py:110
  11.5 163.6 %all-gather.3.cloned.1.call-start = ((), (), s32[]{:S(2)}) async-start(), calls=%async_computation.6 | async-start | bytes 4325376 | tf_op jit(solution)/shard_map/all_gather | solution.py:111
  60.0 9.4 %copy-start.8 = (s32[1,1,512]{2,1,0:T(1,128)S(1)}, s32[1,1,512]{2,1,0:T(1,128)}, u32[]{:S(2)}) copy-start(s32[1,1,512]{2,1,0:T(1,128)} %param.16) | copy-start | bytes 6148
  60.0 9.7 %copy-start.6 = (s32[1,128,4]{1,2,0:T(4,128)S(1)}, s32[1,128,4]{1,2,0:T(4,128)}, u32[]{:S(2)}) copy-start(s32[1,128,4]{1,2,0:T(4,128)} %param.17) | copy-start | bytes 6148
  63.1 61.8 %all-to-all-start.2 = ((bf16[32,16,2,512]{3,2,1,0:T(2,128)(2,1)}), bf16[32,16,2,512]{3,2,1,0:T(2,128)(2,1)S(1)}, u32[]{:S(2)}, u32[]{:S(2)}) async-start(bf16[32,16,2,512]{3,2,1,0:T(2,128)(2,1)} %broadcast_select_fusion), calls=%async_computation.2 | async-start | bytes 2097152 | tf_op jit(solution)/shard_map/all_to_all | solution.py:154
  126.9 20.2 %all-to-all-start.3 = ((bf16[32,16,2,512]{3,2,0,1:T(2,128)(2,1)}), bf16[32,16,2,512]{3,2,0,1:T(2,128)(2,1)S(1)}, u32[]{:S(2)}, u32[]{:S(2)}) async-start(bf16[32,16,2,512]{3,2,0,1:T(2,128)(2,1)} %copy.55), calls=%async_computation.3 | async-start | bytes 2097152 | tf_op jit(solution)/shard_map/all_to_all | solution.py:153
  149.2 2.3 copy-start.3
  151.5 2.6 copy-start.4
  154.1 2.7 copy-start.9
  188.5 4.8 %copy-start.2 = (f32[1024,512]{0,1:T(8,128)S(1)}, f32[1024,512]{0,1:T(8,128)}, u32[]{:S(2)}) copy-start(f32[1024,512]{0,1:T(8,128)} %get-tuple-element.12) | copy-start | bytes 6291460
  193.2 1.2 copy-start.5
  194.5 2.2 copy-start.10
  317.2 38.1 %all-to-all-start.5 = ((f32[32,16,2,512]{3,2,0,1:T(2,128)}), f32[32,16,2,512]{3,2,0,1:T(2,128)}, u32[]{:S(2)}, u32[]{:S(2)}) async-start(f32[32,16,2,512]{3,2,0,1:T(2,128)} %copy.58), calls=%async_computation.5 | async-start | bytes 4194304 | tf_op jit(solution)/shard_map/all_to_all | solution.py:169
Sparse Core Ops, SparseCore 0:
  11.6 88.1 all-gather.4
  102.4 72.6 all-gather.2
where the time goes:
time: 374 us; the launch traced here: 373 us
  blocking collectives  150 us (40%)
  waiting for transfers between devices  116 us (31%)
  local copies, waits for them, and re-layouts  41.1 us (11%)
  matrix products  29.7 us (8%)
  starting transfers between devices  16.9 us (5%)
  between operations  14.3 us (4%)
  other arithmetic  5.61 us (2%)
    all_to_all x1, blocking collectives, on_device(): lax.all_to_all(outgoing, 'seq', split_axis=0, concat_axis=0, tiled=True)  108 us
    all_to_all x1, waiting for transfers between devices, on_device(): lax.all_to_all(answer, 'seq', split_axis=0, concat_axis=0, tiled=True)  55.1 us
    all_to_all x1, waiting for transfers between devices, on_device(): lax.all_to_all(lax.all_to_all(outgoing, 'seq', split_axis=0, concat_axis=...  31.2 us
    all_to_all x1, blocking collectives, on_device(): lax.all_to_all(wanted.reshape(seq_count, item_count, capacity), 'seq', sp...  28.7 us
    all_gather x1, waiting for transfers between devices, on_device(): value_piece = lax.all_gather(value_rows, 'seq', axis=0, tiled=True)  18.3 us
    all_to_all x1, blocking collectives, on_device(): lax.all_to_all(lax.all_to_all(wanted.reshape(seq_count, item_count, capac...  13 us
    all_to_all x1, waiting for transfers between devices, on_device(): lax.all_to_all(lax.all_to_all(answer, 'seq', split_axis=0, concat_axis=0,...  11 us
  transfers between devices with their start and end apart: 5, of which 4 were waited for; matrix products, arithmetic and copies ran while one was open for 7% of the time, Pallas kernels for 0%

commit v1 on v0

v1 whole, which is shorter than its diff:
```python
import jax
import jax.numpy as jnp
from jax import lax
from jax.experimental import pallas as pl
from jax.experimental.pallas import tpu as pltpu
from jax.sharding import Mesh
from jax.sharding import PartitionSpec as P

HEADS = 4
DQK = 64
TOK = 128
WIDTH = 512
HIDDEN = 1024
CHIPS = 16
HALF = CHIPS * TOK
PACK_ROWS = 136
SEND_ROWS = 136
CODE_SCALE = 4096.0

inverse_sharpness = 50.0
norm_eps = 1e-05
unit_eps = 1e-06

BF = jnp.bfloat16
F32 = jnp.float32
VMEM_LIMIT = 56 * 1024 * 1024

NN = (((1,), (0,)), ((), ()))
NT = (((1,), (1,)), ((), ()))


def dot(left, right, contract=NN):
    return lax.dot_general(left, right, contract, preferred_element_type=F32)


def half_silu(half):
    return half + half * jnp.tanh(half)


def silu(inputs):
    return half_silu(0.5 * inputs)


def split_product(left, weight):
    high = left.astype(BF)
    low = (left - high.astype(F32)).astype(BF)
    return dot(high, weight, NT) + dot(low, weight, NT)


def call(kernel, out_shape, n_smem, n_vmem, scratch=()):
    space = [pl.BlockSpec(memory_space=pltpu.SMEM)] * n_smem
    space += [pl.BlockSpec(memory_space=pltpu.VMEM)] * n_vmem
    return pl.pallas_call(
        kernel,
        out_shape=out_shape,
        in_specs=space,
        out_specs=jax.tree.map(lambda _: pl.BlockSpec(memory_space=pltpu.VMEM), out_shape),
        scratch_shapes=list(scratch),
        compiler_params=pltpu.CompilerParams(vmem_limit_bytes=VMEM_LIMIT),
    )


def embed_kernel(table_ref, w_in_ref, w_out_ref, hidden_in_ref, raw_ref, embedding_ref):
    hidden_in = dot(table_ref[...], w_in_ref[...])
    hidden_in_ref[...] = hidden_in
    raw = dot(silu(hidden_in).astype(BF), w_out_ref[...])
    raw_ref[...] = raw
    inv_norm = lax.rsqrt(jnp.sum(raw * raw, axis=-1, keepdims=True) + unit_eps)
    embedding_ref[...] = (raw * inv_norm).astype(BF)


def tower_kernel(
    place_ref, history_ref, w_in_ref, w_out_ref, user_ref, key_scr, value_scr, query_scr, total_scr
):
    parity = place_ref[0]

    def project(step, carry):
        rows = history_ref[step].reshape(2 * TOK, WIDTH)
        at = pl.ds(pl.multiple_of(step * 2 * TOK, 2 * TOK), 2 * TOK)
        value_scr[at, :] = silu(dot(rows, w_in_ref[:, 512:1024])).astype(BF)
        key_scr[at, :] = silu(dot(rows, w_in_ref[:, 1280:1536])).astype(BF)
        return carry

    lax.fori_loop(0, CHIPS, project, 0)

    def own_rows(pair):
        first = history_ref[2 * pair, parity]
        second = history_ref[2 * pair + 1, parity]
        return jnp.concatenate([first, second], axis=0)

    lane = lax.broadcasted_iota(jnp.int32, (2 * TOK, 2 * DQK), 1)
    row = lax.broadcasted_iota(jnp.int32, (2 * TOK, 4 * TOK), 0)
    key_at = lax.broadcasted_iota(jnp.int32, (2 * TOK, 4 * TOK), 1)
    in_second = (row >= TOK).astype(jnp.int32)
    limit = (2 * in_second + parity) * TOK + row - in_second * TOK
    allowed = key_at <= limit

    def attend(pair, carry):
        rows = own_rows(pair)
        query = (silu(dot(rows, w_in_ref[:, 1024:1280])).astype(BF) * 0.0625).astype(BF)
        for head in range(HEADS):
            both = query[:, (head // 2) * 2 * DQK : (head // 2 + 1) * 2 * DQK]
            mine = (lane >= DQK) if head % 2 else (lane < DQK)
            query_scr[head] = jnp.where(mine, both, jnp.zeros_like(both))
        total_scr[...] = jnp.zeros_like(total_scr)

        def tile(step, masked):
            at = pl.ds(pl.multiple_of(step * 4 * TOK, 4 * TOK), 4 * TOK)
            for head in range(HEADS):
                keys = key_scr[at, (head // 2) * 2 * DQK : (head // 2 + 1) * 2 * DQK]
                weights = half_silu(dot(query_scr[head], keys, NT))
                if masked:
                    weights = jnp.where(allowed, weights, 0.0)
                values = value_scr[at, head * 128 : (head + 1) * 128]
                total_scr[:, head * 128 : (head + 1) * 128] += dot(weights.astype(BF), values)

        def full(step, inner):
            tile(step, False)
            return inner

        lax.fori_loop(0, pair, full, 0)
        tile(pair, True)

        attended = total_scr[...]
        centered = attended - jnp.mean(attended, axis=-1, keepdims=True)
        variance = jnp.mean(centered * centered, axis=-1, keepdims=True)
        normed = centered * lax.rsqrt(variance + norm_eps)
        gate_units = silu(dot(rows, w_in_ref[:, 0:512]))
        mixed_rows = (normed * gate_units).astype(BF)
        updated = rows.astype(F32) + dot(mixed_rows, w_out_ref[...])
        scale = lax.rsqrt(jnp.sum(updated * updated, axis=-1, keepdims=True) + unit_eps)
        at = pl.ds(pl.multiple_of(pair * 2 * TOK, 2 * TOK), 2 * TOK)
        user_ref[at, :] = (updated * scale).astype(BF)
        return carry

    lax.fori_loop(0, CHIPS // 2, attend, 0)


def label_places(labels_ref, block, entry, chip):
    label = labels_ref[block : block + 1, entry * TOK : (entry + 1) * TOK].astype(jnp.int32)
    local = label - chip * 64
    inside = (label >= 0) & (local >= 0) & (local < 64)
    return jnp.where(inside, (local & 1) * 32 + (local >> 1), -1)


def scores_kernel(
    place_ref, table_ref, user_ref, rows_ref, used_ref, labels_ref,
    exps_ref, hits_ref, exchange_ref, entry_scr,
):
    chip = place_ref[1]
    row_ids = lax.broadcasted_iota(jnp.int32, (32, TOK), 1).astype(F32)
    for owner in range(32):
        pick = (row_ids == rows_ref[:, owner : owner + 1]).astype(BF)
        rows = dot(pick, table_ref[owner * TOK : (owner + 1) * TOK, :])
        for slot in range(2):
            for part in range(4):
                entry_scr[part, pl.ds(slot * 32 + owner, 16, stride=64), :] = rows[
                    slot * 16 : (slot + 1) * 16, part * 128 : (part + 1) * 128
                ]
    slot_ids = lax.broadcasted_iota(jnp.int32, (64, TOK), 0)
    exchange_ref[...] = jnp.zeros_like(exchange_ref)
    for block in range(CHIPS):
        entries = jnp.concatenate(
            [entry_scr[part, block * 64 : (block + 1) * 64, :] for part in range(4)], axis=1
        ).astype(BF)
        scores = dot(entries, user_ref[block * TOK : (block + 1) * TOK, :], NT) * inverse_sharpness
        used = used_ref[:, block : block + 1] >= 0.0
        exps = jnp.where(used, jnp.exp(scores), 0.0)
        exps_ref[block] = exps
        hits = jnp.zeros((64, TOK), F32)
        for entry in range(4):
            place = label_places(labels_ref, block, entry, chip)
            hits = hits + (slot_ids == place).astype(F32)
        hits_ref[block] = hits
        total = jnp.sum(exps, axis=0, keepdims=True)
        exchange_ref[:, block : block + 1, :] = jnp.broadcast_to(total[None], (CHIPS, 1, TOK))
        exchange_ref[block, 16:17, :] = jnp.sum(hits * scores, axis=0, keepdims=True)


def gradient_kernel(
    place_ref, exps_ref, hits_ref, user_ref, exchange_ref, labels_ref, index_ref,
    send_ref, loss_ref, grad_scr,
):
    chip = place_ref[1]
    sums = jnp.sum(exchange_ref[...], axis=0)
    positives = jnp.zeros((CHIPS, TOK), F32)
    for entry in range(4):
        positives = positives + (labels_ref[:, entry * TOK : (entry + 1) * TOK] >= 0.0).astype(F32)
    divisor = jnp.maximum(positives, 1.0)
    totals = sums[0:16]
    own = lax.broadcasted_iota(jnp.int32, (CHIPS, TOK), 0) == chip
    losses = (positives * jnp.log(totals) - sums[16:17]) / divisor
    loss_ref[...] = jnp.sum(jnp.where(own, losses, 0.0), axis=0, keepdims=True)
    exp_scale = positives / (divisor * totals)
    hit_scale = 1.0 / divisor
    for block in range(CHIPS):
        score_grad = (
            exps_ref[block] * exp_scale[block : block + 1]
            - hits_ref[block] * hit_scale[block : block + 1]
        ).astype(BF)
        grads = dot(score_grad, user_ref[block * TOK : (block + 1) * TOK, :]) * inverse_sharpness
        for slot in range(2):
            for part in range(4):
                at = part * 32 + slot * 16 + block
                grad_scr[pl.ds(at, 32, stride=SEND_ROWS), :] = grads[
                    slot * 32 : (slot + 1) * 32, part * 128 : (part + 1) * 128
                ]
    zeros = jnp.zeros((32, TOK), F32)
    for extra in range(8):
        grad_scr[pl.ds(TOK + extra, 32, stride=SEND_ROWS), :] = index_ref[...] if extra == 0 else zeros
    send_ref[...] = grad_scr[...].astype(BF)


def owner_kernel(
    arrived_ref, index_ref, hidden_in_ref, raw_ref, w_in_ref, w_out_ref, gradient_ref, rows_scr
):
    row_ids = lax.broadcasted_iota(jnp.int32, (TOK, TOK), 0).astype(F32)
    row_grad = jnp.zeros((TOK, WIDTH), F32)
    for group in range(8):
        index = jnp.zeros((1, TOK), F32)
        for member in range(4):
            sender = group * 4 + member
            index = index + index_ref[sender : sender + 1, :]
            for part in range(4):
                rows_scr[member * 32 : (member + 1) * 32, part * 128 : (part + 1) * 128] = arrived_ref[
                    sender, part * 32 : (part + 1) * 32, :
                ]
        pick = (row_ids == index).astype(BF)
        row_grad = row_grad + dot(pick, rows_scr[...])
    raw = raw_ref[...]
    inv_norm = lax.rsqrt(jnp.sum(raw * raw, axis=-1, keepdims=True) + unit_eps)
    unit = raw * inv_norm
    raw_grad = (row_grad - unit * jnp.sum(unit * row_grad, axis=-1, keepdims=True)) * inv_norm
    hidden_grad = split_product(raw_grad, w_out_ref[...])
    hidden_in = hidden_in_ref[...]
    sigma = 0.5 * jnp.tanh(0.5 * hidden_in) + 0.5
    input_grad = hidden_grad * (sigma * (1.0 + hidden_in * (1.0 - sigma)))
    gradient_ref[...] = split_product(input_grad, w_in_ref[...])


def on_device(
    history, w_in, w_out, item_table, w_item_in, w_item_out, req_rows, req_counts, labels
):
    chip = lax.axis_index("z")
    core = lax.axis_index("core")
    place = jnp.stack([core, chip]).astype(jnp.int32)

    with jax.named_scope("embed"):
        hidden_in, raw_embed, embedding = call(
            embed_kernel,
            (
                jax.ShapeDtypeStruct((TOK, HIDDEN), F32),
                jax.ShapeDtypeStruct((TOK, WIDTH), F32),
                jax.ShapeDtypeStruct((TOK, WIDTH), BF),
            ),
            0,
            3,
        )(item_table, w_item_in, w_item_out)

    with jax.named_scope("pack"):
        wanted = req_rows[0, 0]
        used = jnp.arange(2, dtype=jnp.int32)[None, :] < req_counts[0, 0][:, None]
        wanted = jnp.where(used, wanted, -1)
        packed = jnp.concatenate(
            [
                (history[0].astype(F32) * CODE_SCALE).astype(jnp.float16),
                wanted.reshape(2, WIDTH).astype(jnp.float16),
                labels[0].T.reshape(1, WIDTH).astype(jnp.float16),
                jnp.zeros((PACK_ROWS - TOK - 3, WIDTH), jnp.float16),
            ],
            axis=0,
        )
        packed, embedding = lax.optimization_barrier((packed, embedding))

    with jax.named_scope("table_gather"):
        table = lax.all_gather(embedding, ("core", "item"), axis=0, tiled=True)

    with jax.named_scope("history_gather"):
        gathered = lax.all_gather(packed, ("z", "core"), axis=0, tiled=True)

    with jax.named_scope("unpack"):
        gathered = gathered.reshape(CHIPS, 2, PACK_ROWS, WIDTH)
        histories = (gathered[:, :, :TOK].astype(F32) * (1.0 / CODE_SCALE)).astype(BF)
        extras = lax.dynamic_slice(
            gathered, (0, core, TOK, 0), (CHIPS, 1, 8, WIDTH)
        ).reshape(CHIPS, 8, WIDTH).astype(F32)
        label_rows = extras[:, 2]
        asked = lax.dynamic_slice(extras[:, 0:2].reshape(CHIPS, 1024), (0, chip * 64), (CHIPS, 64))
        asked = asked.reshape(CHIPS, 32, 2)
        by_owner = asked.transpose(2, 0, 1).reshape(32, 32)
        by_block = asked.transpose(2, 1, 0).reshape(64, CHIPS)
        sender = core * 16 + lax.axis_index("item")
        quarter = (jnp.arange(4) == sender % 4).astype(F32)
        index = (by_owner.T[:, None, :] * quarter[None, :, None]).reshape(32, TOK)

    with jax.named_scope("tower"):
        user_rows = call(
            tower_kernel,
            jax.ShapeDtypeStruct((HALF, WIDTH), BF),
            1,
            3,
            [
                pltpu.VMEM((2 * HALF, HEADS * DQK), BF),
                pltpu.VMEM((2 * HALF, WIDTH), BF),
                pltpu.VMEM((HEADS, 2 * TOK, 2 * DQK), BF),
                pltpu.VMEM((2 * TOK, WIDTH), F32),
            ],
        )(place, histories, w_in, w_out)

    with jax.named_scope("scores"):
        exps, hits, exchange = call(
            scores_kernel,
            (
                jax.ShapeDtypeStruct((CHIPS, 64, TOK), F32),
                jax.ShapeDtypeStruct((CHIPS, 64, TOK), F32),
                jax.ShapeDtypeStruct((CHIPS, 24, TOK), F32),
            ),
            1,
            5,
            [pltpu.VMEM((4, 1024, 128), F32)],
        )(place, table, user_rows, by_owner, by_block, label_rows)

    with jax.named_scope("totals_exchange"):
        exchange = lax.all_to_all(exchange, "z", split_axis=0, concat_axis=0, tiled=True)

    with jax.named_scope("gradient_rows"):
        send, loss = call(
            gradient_kernel,
            (
                jax.ShapeDtypeStruct((32 * SEND_ROWS, 128), BF),
                jax.ShapeDtypeStruct((1, TOK), F32),
            ),
            1,
            6,
            [pltpu.VMEM((32 * SEND_ROWS, 128), F32)],
        )(place, exps, hits, user_rows, exchange, label_rows, index)

    with jax.named_scope("gradient_send"):
        arrived = lax.all_to_all(
            send.reshape(32, SEND_ROWS, 128), ("core", "item"), split_axis=0, concat_axis=0, tiled=True
        )

    with jax.named_scope("owner"):
        gradient = call(
            owner_kernel,
            jax.ShapeDtypeStruct((TOK, WIDTH), F32),
            0,
            6,
            [pltpu.VMEM((TOK, WIDTH), BF)],
        )(arrived, arrived[:, TOK].astype(F32), hidden_in, raw_embed, w_item_in, w_item_out)
    return (loss, gradient)


def solution(mesh):
    split = Mesh(mesh.devices.reshape(CHIPS, 2, 16), ("z", "core", "item"))
    rows = ("z", "core")
    placed = (
        P("item", rows, None),
        P(),
        P(),
        P(("z", "core", "item"), None),
        P(),
        P(),
        P("item", rows, None, None),
        P("item", rows, None),
        P("item", rows, None),
    )
    return jax.shard_map(
        on_device,
        mesh=split,
        in_specs=placed,
        out_specs=(P("item", rows), P(("z", "core", "item"), None)),
        check_vma=False,
    )
```

time: 374 us -> 206 us (0.55)
  waiting for transfers between devices: 116 us -> 12.2 us
  Pallas kernels: 0 us -> 73.7 us
  blocking collectives: 150 us -> 81.1 us
  local copies, waits for them, and re-layouts: 41.1 us -> 7.55 us
  matrix products: 29.7 us -> 0 us
  starting transfers between devices: 16.9 us -> 6.52 us
  other arithmetic: 5.61 us -> 10.5 us
    all_to_all x3 -> x1, blocking collectives: 150 us -> 28.5 us  [on_device(): lax.all_to_all(send.reshape(32, SEND_ROWS, 128), ('core', 'item'), split_...]
    all_to_all x3 -> x1, waiting for transfers between devices: 97.4 us -> 12.2 us  [on_device(): lax.all_to_all(exchange, 'z', split_axis=0, concat_axis=0, tiled=True)]
    pallas_call x0 -> x5, Pallas kernels: none -> 73.7 us  [the longest x1 54.8 us: on_device(): call(tower_kernel, jax.ShapeDtypeStruct((HALF, WIDTH), BF), 1, 3, [pltpu....]
    all_gather x0 -> x1, blocking collectives: none -> 52.6 us  [on_device(): gathered = lax.all_gather(packed, ('z', 'core'), axis=0, tiled=True)]
    dot_general x12 -> x0, matrix products: 29.7 us -> none  [the longest x1 6.71 us: on_device(): jnp.einsum('hqk,khd->qhd', weights, value_heads, preferred_element_type=j...]
    all_gather x2 -> x1, waiting for transfers between devices: 18.3 us -> 0.01 us  [on_device(): table = lax.all_gather(embedding, ('core', 'item'), axis=0, tiled=True)]
    reshape x7 -> x1, local copies, waits for them, and re-layouts: 16.4 us -> 0.01 us  [on_device(): extras[:, 0:2].reshape(CHIPS, 1024)]
    all_to_all x6 -> x0, local copies, waits for them, and re-layouts: 10.8 us -> none  [the longest x1 4.08 us: on_device(): lax.all_to_all(lax.all_to_all(outgoing, 'seq', split_axis=0, concat_axis=...]
  transfers between devices with their start and end apart: 5 -> 2, of which waited for: 4 -> 1; matrix products, arithmetic and copies ran while one was open for 7% -> 4% of each run, Pallas kernels for 0% -> 27%
where the time goes in v1:
time: 206 us
  blocking collectives  81.1 us (39%)
  Pallas kernels  73.7 us (36%)
  between operations  14.2 us (7%)
  waiting for transfers between devices  12.2 us (6%)
  other arithmetic  10.5 us (5%)
  local copies, waits for them, and re-layouts  7.55 us (4%)
  starting transfers between devices  6.52 us (3%)
    pallas_call x1, Pallas kernels, on_device(): call(tower_kernel, jax.ShapeDtypeStruct((HALF, WIDTH), BF), 1, 3, [pltpu....  54.8 us
    all_gather x1, blocking collectives, on_device(): gathered = lax.all_gather(packed, ('z', 'core'), axis=0, tiled=True)  52.6 us
    all_to_all x1, blocking collectives, on_device(): lax.all_to_all(send.reshape(32, SEND_ROWS, 128), ('core', 'item'), split_...  28.5 us
    all_to_all x1, waiting for transfers between devices, on_device(): lax.all_to_all(exchange, 'z', split_axis=0, concat_axis=0, tiled=True)  12.2 us
    pallas_call x1, Pallas kernels, on_device(): call(scores_kernel, (jax.ShapeDtypeStruct((CHIPS, 64, TOK), F32), jax.Sha...  7.2 us
    all_to_all x1, starting transfers between devices, on_device(): lax.all_to_all(exchange, 'z', split_axis=0, concat_axis=0, tiled=True)  6.48 us
    convert_element_type x1, other arithmetic, on_device(): (gathered[:, :, :TOK].astype(F32) * (1.0 / CODE_SCALE)).astype(BF)  5.55 us
    pallas_call x1, Pallas kernels, on_device(): call(owner_kernel, jax.ShapeDtypeStruct((TOK, WIDTH), F32), 0, 6, [pltpu....  4.94 us
  transfers between devices with their start and end apart: 2, of which 1 were waited for; matrix products, arithmetic and copies ran while one was open for 4% of the time, Pallas kernels for 27%

profile of v1, /device:TPU:1, one launch (start us, length us, event | category | flops | bytes accessed | tf_op | source)
XLA Modules:
  0.0 205.8 jit_solution(687934613802064611)
XLA Ops:
  7.2 0.5 broadcast.20
  7.7 1.3 reduce.3
  9.4 0.8 copy.24
  10.6 0.9 fusion
  11.5 0.7 convert_bitcast_fusion
  12.3 2.9 %embed.1 = (f32[128,1024]{1,0:T(8,128)}, f32[128,512]{1,0:T(8,128)}, bf16[128,512]{1,0:T(8,128)(2,1)}) custom-call(bf16[128,512]{1,0:T(8,128)(2,1)} %table_ref.1, bf16[512,1024]{1,0:T(8,128)(2,1)} %w_in_ref.5, bf16[1024,512]{1,0:T(8,128)(2,1)} %w_out_ref.5), custom_call_target="tpu_custom_call" | custom-call | tf_op jit(solution)/shard_map/embed/pallas_call | solution.py:249
  15.3 52.6 %all-gather.4 = f16[4352,512]{1,0:T(8,128)(2,1)S(1)} all-gather(f16[136,512]{1,0:T(8,128)(2,1)S(1)} %maximum_maximum_fusion), channel_id=1, replica_groups=mesh['z'=16,'core'=2,'item'=16] {'z','core'}, dimensions={0}, use_global_device_ids=true | all-gather | bytes 4595712 | tf_op jit(solution)/shard_map/history_gather/all_gather | solution.py:279
  68.0 2.0 copy-done
  70.3 0.7 copy.28
  70.9 0.6 copy.29
  71.6 0.6 pad_add_fusion.place_ref
  72.1 5.5 %multiply_convert_fusion.history_ref = bf16[16,2,128,512]{3,2,1,0:T(8,128)(2,1)} fusion(f16[16,2,136,512]{3,2,1,0:T(8,128)(2,1)} %bitcast.42), kind=kLoop, calls=%fused_computation | loop fusion | flops 6291456 | bytes 8388608 | tf_op jit(solution)/shard_map/unpack/convert_element_type | solution.py:283
  77.7 54.8 %tower.1.user_ref = bf16[2048,512]{1,0:T(8,128)(2,1)} custom-call(s32[2]{0:T(128)} %pad_add_fusion.place_ref, bf16[16,2,128,512]{3,2,1,0:T(8,128)(2,1)} %multiply_convert_fusion.history_ref, bf16[512,1536]{1,0:T(8,128)(2,1)} %w_in_ref.4, bf16[512,512]{1,0:T(8,128)(2,1)} %w_out_ref.4), custom_call_target="tpu_custom_call" | custom-call | tf_op jit(solution)/shard_map/tower/pallas_call | solution.py:297
  132.4 0.6 slice_bitcast_fusion.1.labels_ref
  133.1 7.2 %scores.1 = (f32[16,64,128]{2,1,0:T(8,128)}, f32[16,64,128]{2,1,0:T(8,128)}, f32[16,24,128]{2,1,0:T(8,128)}) custom-call(s32[2]{0:T(128)} %pad_add_fusion.place_ref, bf16[4096,512]{1,0:T(8,128)(2,1)} %all-gather.3.cloned.1.call-done.table_ref, bf16[2048,512]{1,0:T(8,128)(2,1)} %tower.1.user_ref, f32[32,32]{1,0:T(8,128)} %bitcast.46, f32[64,16]{1,0:T(8,128)} %bitcast.48, ...), custom_call_target="tpu_custom_call" | custom-call | tf_op jit(solution)/shard_map/scores/pallas_call | solution.py:311
  140.3 6.5 %all-to-all-start = ((f32[16,24,128]{2,1,0:T(8,128)}), f32[16,24,128]{2,1,0:T(8,128)S(1)}, u32[]{:S(2)}, u32[]{:S(2)}) async-start(f32[16,24,128]{2,1,0:T(8,128)} %get-tuple-element.17), calls=%async_computation | async-start | bytes 393216 | tf_op jit(solution)/shard_map/totals_exchange/all_to_all | solution.py:324
  147.1 0.6 broadcast_multiply_fusion.index_ref
  147.7 12.2 %all-to-all-done.exchange_ref = f32[16,24,128]{2,1,0:T(8,128)S(1)} async-done(((f32[16,24,128]{2,1,0:T(8,128)}), f32[16,24,128]{2,1,0:T(8,128)S(1)}, u32[]{:S(2)}, u32[]{:S(2)}) %all-to-all-start) | async-done | bytes 196640 | tf_op jit(solution)/shard_map/totals_exchange/all_to_all | solution.py:324
  159.9 0.7 copy-done.2
  160.6 3.9 %gradient_rows.1 = (bf16[4352,128]{1,0:T(8,128)(2,1)}, f32[1,128]{1,0:T(1,128)}) custom-call(s32[2]{0:T(128)} %pad_add_fusion.place_ref, f32[16,64,128]{2,1,0:T(8,128)} %get-tuple-element.15.exps_ref, f32[16,64,128]{2,1,0:T(8,128)} %get-tuple-element.16.hits_ref, bf16[2048,512]{1,0:T(8,128)(2,1)} %tower.1.user_ref, f32[16,24,128]{2,1,0:T(8,128)} %copy-done.2, ...), custom_call_target="tpu_custom_call" | custom-call | tf_op jit(solution)/shard_map/gradient_rows/pallas_call | solution.py:327
  164.5 28.5 %all_to_all.10.arrived_ref = bf16[32,136,128]{2,1,0:T(8,128)(2,1)S(1)} all-to-all(bf16[32,136,128]{2,1,0:T(8,128)(2,1)} %bitcast.43), channel_id=1, replica_groups=mesh['z'=16,'core'=2,'item'=16] {'core','item'}, dimensions={0} | all-to-all | bytes 2228224 | tf_op jit(solution)/shard_map/gradient_send/all_to_all | solution.py:339
  193.0 0.7 fusion.2.index_ref
  193.7 0.3 copy-done.1
  194.0 4.9 %owner.1 = f32[128,512]{1,0:T(8,128)} custom-call(bf16[32,136,128]{2,1,0:T(8,128)(2,1)} %copy-done.1, f32[32,128]{1,0:T(8,128)} %fusion.2.index_ref, f32[128,1024]{1,0:T(8,128)} %get-tuple-element.20.hidden_in_ref, f32[128,512]{1,0:T(8,128)} %get-tuple-element.21.raw_ref, bf16[512,1024]{1,0:T(8,128)(2,1)} %w_in_ref.5, bf16[1024,512]{1,0:T(8,128)(2,1)} %w_out_ref.5), custom_call_target="tpu_custom_call" | custom-call | tf_op jit(solution)/shard_map/owner/pallas_call | solution.py:344
  (32 shorter events, 1.5 us)
Async XLA Ops:
  7.2 125.9 %all-gather.3.cloned.1.call-start = ((), (), s32[]{:S(2)}) async-start(), calls=%async_computation.2 | async-start | bytes 4325376 | tf_op jit(solution)/shard_map/table_gather/all_gather | solution.py:276
  68.0 2.0 copy-start
  132.4 14.5 %copy-start.3 = (f32[2,16,32]{2,1,0:T(8,128)S(1)}, f32[2,16,32]{2,1,0:T(8,128)}, u32[]{:S(2)}) copy-start(f32[2,16,32]{2,1,0:T(8,128)} %copy.28) | copy-start | bytes 12292
  140.3 19.7 %all-to-all-start = ((f32[16,24,128]{2,1,0:T(8,128)}), f32[16,24,128]{2,1,0:T(8,128)S(1)}, u32[]{:S(2)}, u32[]{:S(2)}) async-start(f32[16,24,128]{2,1,0:T(8,128)} %get-tuple-element.17), calls=%async_computation | async-start | bytes 393216 | tf_op jit(solution)/shard_map/totals_exchange/all_to_all | solution.py:324
  159.9 0.7 copy-start.2
  193.0 1.0 copy-start.1
Sparse Core Ops, SparseCore 0:
  15.4 67.1 all-gather.2

commit v2 on v1

--- a/solution.py
+++ b/solution.py
@@ -13,9 +13,11 @@
 HIDDEN = 1024
 CHIPS = 16
 HALF = CHIPS * TOK
-PACK_ROWS = 136
+TILE = 512
+PACK_ROWS = 144
 SEND_ROWS = 136
-CODE_SCALE = 4096.0
+RANGE = 6.0
+CODES = 32760.0
 
 inverse_sharpness = 50.0
 norm_eps = 1e-05
@@ -60,7 +62,22 @@
     )
 
 
-def embed_kernel(table_ref, w_in_ref, w_out_ref, hidden_in_ref, raw_ref, embedding_ref):
+def prepare_kernel(
+    history_ref, wanted_ref, counts_ref, labels_ref, table_ref, w_in_ref, w_out_ref,
+    packed_ref, hidden_in_ref, raw_ref, embedding_ref,
+):
+    rows = history_ref[...].astype(F32)
+    root = jnp.exp(jnp.log(jnp.abs(rows) * (1.0 / RANGE)) * (1.0 / 3.0)) * CODES
+    codes = jnp.where(rows < 0.0, -root, root)
+    packed_ref[0:TOK, :] = jnp.round(codes).astype(jnp.int32).astype(jnp.int16)
+    wanted = wanted_ref[...]
+    slot = lax.broadcasted_iota(jnp.int32, (2, WIDTH), 0)
+    wanted = jnp.where(slot < counts_ref[...], wanted, -1)
+    labels = jnp.concatenate([labels_ref[entry : entry + 1, :] for entry in range(4)], axis=1)
+    at = lax.broadcasted_iota(jnp.int32, (16, WIDTH), 0)
+    extras = jnp.where(at == 0, wanted[0:1], jnp.where(at == 1, wanted[1:2], labels))
+    packed_ref[TOK:PACK_ROWS, :] = extras.astype(jnp.int16)
+
     hidden_in = dot(table_ref[...], w_in_ref[...])
     hidden_in_ref[...] = hidden_in
     raw = dot(silu(hidden_in).astype(BF), w_out_ref[...])
@@ -69,57 +86,80 @@
     embedding_ref[...] = (raw * inv_norm).astype(BF)
 
 
+def decode(codes):
+    root = codes.astype(F32) * (RANGE ** (1.0 / 3.0) / CODES)
+    return (root * root * root).astype(BF)
+
+
 def tower_kernel(
-    place_ref, history_ref, w_in_ref, w_out_ref, user_ref, key_scr, value_scr, query_scr, total_scr
+    place_ref, packed_ref, w_in_ref, w_out_ref, user_ref, rows_ref, labels_ref,
+    key_scr, value_scr, query_scr, total_scr,
 ):
     parity = place_ref[0]
+    chip = place_ref[1]
+
+    for block in range(CHIPS):
+        extras = packed_ref[block, parity, TOK:PACK_ROWS, :].astype(F32)
+        mine = pltpu.roll(extras, WIDTH - chip * 32, 1)
+        rows_ref[block : block + 1, :] = mine[0:1, 0:TOK]
+        rows_ref[CHIPS + block : CHIPS + block + 1, :] = mine[1:2, 0:TOK]
+        labels_ref[block : block + 1, :] = extras[2:3]
 
     def project(step, carry):
-        rows = history_ref[step].reshape(2 * TOK, WIDTH)
-        at = pl.ds(pl.multiple_of(step * 2 * TOK, 2 * TOK), 2 * TOK)
+        pieces = [packed_ref[2 * step + n // 2, n % 2, 0:TOK, :] for n in range(4)]
+        rows = decode(jnp.concatenate(pieces, axis=0))
+        at = pl.ds(pl.multiple_of(step * TILE, TILE), TILE)
         value_scr[at, :] = silu(dot(rows, w_in_ref[:, 512:1024])).astype(BF)
-        key_scr[at, :] = silu(dot(rows, w_in_ref[:, 1280:1536])).astype(BF)
+        key_scr[:, at] = silu(dot(w_in_ref[:, 1280:1536], rows, (((0,), (1,)), ((), ())))).astype(BF)
         return carry
 
-    lax.fori_loop(0, CHIPS, project, 0)
-
-    def own_rows(pair):
-        first = history_ref[2 * pair, parity]
-        second = history_ref[2 * pair + 1, parity]
-        return jnp.concatenate([first, second], axis=0)
-
-    lane = lax.broadcasted_iota(jnp.int32, (2 * TOK, 2 * DQK), 1)
-    row = lax.broadcasted_iota(jnp.int32, (2 * TOK, 4 * TOK), 0)
-    key_at = lax.broadcasted_iota(jnp.int32, (2 * TOK, 4 * TOK), 1)
-    in_second = (row >= TOK).astype(jnp.int32)
-    limit = (2 * in_second + parity) * TOK + row - in_second * TOK
-    allowed = key_at <= limit
-
-    def attend(pair, carry):
-        rows = own_rows(pair)
+    lax.fori_loop(0, 2 * HALF // TILE, project, 0)
+
+    lane = lax.broadcasted_iota(jnp.int32, (TILE, 2 * DQK), 1)
+
+    def tile(top, height, start, width, diagonal=None):
+        if diagonal is not None:
+            row = lax.broadcasted_iota(jnp.int32, (height, width), 0)
+            key_at = lax.broadcasted_iota(jnp.int32, (height, width), 1) + diagonal[0]
+            block = row // TOK + diagonal[1]
+            allowed = key_at <= (2 * block + parity) * TOK + row % TOK
+        weights = []
+        for head in range(HEADS):
+            keys = key_scr[(head // 2) * 2 * DQK : (head // 2 + 1) * 2 * DQK, pl.ds(start, width)]
+            weight = half_silu(dot(query_scr[head, top : top + height], keys))
+            if diagonal is not None:
+                weight = jnp.where(allowed, weight, 0.0)
+            weights.append(weight.astype(BF))
+        for head in range(HEADS):
+            values = value_scr[pl.ds(start, width), head * 128 : (head + 1) * 128]
+            total_scr[top : top + height, head * 128 : (head + 1) * 128] += dot(weights[head], values)
+
+    for group in range(HALF // TILE):
+        rows = decode(
+            jnp.concatenate(
+                [packed_ref[4 * group + n, parity, 0:TOK, :] for n in range(4)], axis=0
+            )
+        )
         query = (silu(dot(rows, w_in_ref[:, 1024:1280])).astype(BF) * 0.0625).astype(BF)
         for head in range(HEADS):
             both = query[:, (head // 2) * 2 * DQK : (head // 2 + 1) * 2 * DQK]
             mine = (lane >= DQK) if head % 2 else (lane < DQK)
             query_scr[head] = jnp.where(mine, both, jnp.zeros_like(both))
         total_scr[...] = jnp.zeros_like(total_scr)
-
-        def tile(step, masked):
-            at = pl.ds(pl.multiple_of(step * 4 * TOK, 4 * TOK), 4 * TOK)
-            for head in range(HEADS):
-                keys = key_scr[at, (head // 2) * 2 * DQK : (head // 2 + 1) * 2 * DQK]
-                weights = half_silu(dot(query_scr[head], keys, NT))
-                if masked:
-                    weights = jnp.where(allowed, weights, 0.0)
-                values = value_scr[at, head * 128 : (head + 1) * 128]
-                total_scr[:, head * 128 : (head + 1) * 128] += dot(weights.astype(BF), values)
-
-        def full(step, inner):
-            tile(step, False)
-            return inner
-
-        lax.fori_loop(0, pair, full, 0)
-        tile(pair, True)
+        base = group * 2 * TILE
+
+        def earlier(step, carry):
+            tile(0, TILE, pl.multiple_of(step * TILE, TILE), TILE)
+            return carry
+
+        lax.fori_loop(0, base // TILE, earlier, 0)
+        for pair in range(2):
+            top = pair * 2 * TOK
+            first = base + 2 * top
+            if pair:
+                tile(top, 2 * TOK, base, TILE)
+            tile(top, 2 * TOK, first, 2 * TOK, (0, 0))
+            tile(top + TOK, TOK, first + 2 * TOK, 2 * TOK, (2 * TOK, 1))
 
         attended = total_scr[...]
         centered = attended - jnp.mean(attended, axis=-1, keepdims=True)
@@ -129,11 +169,7 @@
         mixed_rows = (normed * gate_units).astype(BF)
         updated = rows.astype(F32) + dot(mixed_rows, w_out_ref[...])
         scale = lax.rsqrt(jnp.sum(updated * updated, axis=-1, keepdims=True) + unit_eps)
-        at = pl.ds(pl.multiple_of(pair * 2 * TOK, 2 * TOK), 2 * TOK)
-        user_ref[at, :] = (updated * scale).astype(BF)
-        return carry
-
-    lax.fori_loop(0, CHIPS // 2, attend, 0)
+        user_ref[group * TILE : (group + 1) * TILE, :] = (updated * scale).astype(BF)
 
 
 def label_places(labels_ref, block, entry, chip):
@@ -144,15 +180,19 @@
 
 
 def scores_kernel(
-    place_ref, table_ref, user_ref, rows_ref, used_ref, labels_ref,
+    place_ref, table_ref, user_ref, rows_ref, labels_ref,
     exps_ref, hits_ref, exchange_ref, entry_scr,
 ):
     chip = place_ref[1]
     row_ids = lax.broadcasted_iota(jnp.int32, (32, TOK), 1).astype(F32)
     for owner in range(32):
-        pick = (row_ids == rows_ref[:, owner : owner + 1]).astype(BF)
-        rows = dot(pick, table_ref[owner * TOK : (owner + 1) * TOK, :])
+        asked = jnp.broadcast_to(rows_ref[:, owner : owner + 1], (32, TOK))
+        rows = dot((row_ids == asked).astype(BF), table_ref[owner * TOK : (owner + 1) * TOK, :])
+        used = (asked >= 0.0).astype(F32)
         for slot in range(2):
+            entry_scr[4, pl.ds(slot * 32 + owner, 16, stride=64), :] = used[
+                slot * 16 : (slot + 1) * 16
+            ]
             for part in range(4):
                 entry_scr[part, pl.ds(slot * 32 + owner, 16, stride=64), :] = rows[
                     slot * 16 : (slot + 1) * 16, part * 128 : (part + 1) * 128
@@ -164,7 +204,7 @@
             [entry_scr[part, block * 64 : (block + 1) * 64, :] for part in range(4)], axis=1
         ).astype(BF)
         scores = dot(entries, user_ref[block * TOK : (block + 1) * TOK, :], NT) * inverse_sharpness
-        used = used_ref[:, block : block + 1] >= 0.0
+        used = entry_scr[4, block * 64 : (block + 1) * 64, :] > 0.0
         exps = jnp.where(used, jnp.exp(scores), 0.0)
         exps_ref[block] = exps
         hits = jnp.zeros((64, TOK), F32)
@@ -178,7 +218,7 @@
 
 
 def gradient_kernel(
-    place_ref, exps_ref, hits_ref, user_ref, exchange_ref, labels_ref, index_ref,
+    place_ref, exps_ref, hits_ref, user_ref, exchange_ref, labels_ref, rows_ref,
     send_ref, loss_ref, grad_scr,
 ):
     chip = place_ref[1]
@@ -205,9 +245,12 @@
                 grad_scr[pl.ds(at, 32, stride=SEND_ROWS), :] = grads[
                     slot * 32 : (slot + 1) * 32, part * 128 : (part + 1) * 128
                 ]
+    at = lax.broadcasted_iota(jnp.int32, (32, TOK), 0) + (place_ref[2] & 3) * 32
+    spread = (lax.broadcasted_iota(jnp.int32, (32, TOK), 1) == at).astype(BF)
+    index = dot(rows_ref[...].astype(BF), spread, (((0,), (0,)), ((), ())))[0:32]
     zeros = jnp.zeros((32, TOK), F32)
     for extra in range(8):
-        grad_scr[pl.ds(TOK + extra, 32, stride=SEND_ROWS), :] = index_ref[...] if extra == 0 else zeros
+        grad_scr[pl.ds(TOK + extra, 32, stride=SEND_ROWS), :] = zeros if extra else index
     send_ref[...] = grad_scr[...].astype(BF)
 
 
@@ -243,34 +286,23 @@
 ):
     chip = lax.axis_index("z")
     core = lax.axis_index("core")
-    place = jnp.stack([core, chip]).astype(jnp.int32)
-
-    with jax.named_scope("embed"):
-        hidden_in, raw_embed, embedding = call(
-            embed_kernel,
+    place = jnp.stack([core, chip, lax.axis_index("item")]).astype(jnp.int32)
+
+    with jax.named_scope("prepare"):
+        packed, hidden_in, raw_embed, embedding = call(
+            prepare_kernel,
             (
+                jax.ShapeDtypeStruct((PACK_ROWS, WIDTH), jnp.int16),
                 jax.ShapeDtypeStruct((TOK, HIDDEN), F32),
                 jax.ShapeDtypeStruct((TOK, WIDTH), F32),
                 jax.ShapeDtypeStruct((TOK, WIDTH), BF),
             ),
             0,
-            3,
-        )(item_table, w_item_in, w_item_out)
-
-    with jax.named_scope("pack"):
-        wanted = req_rows[0, 0]
-        used = jnp.arange(2, dtype=jnp.int32)[None, :] < req_counts[0, 0][:, None]
-        wanted = jnp.where(used, wanted, -1)
-        packed = jnp.concatenate(
-            [
-                (history[0].astype(F32) * CODE_SCALE).astype(jnp.float16),
-                wanted.reshape(2, WIDTH).astype(jnp.float16),
-                labels[0].T.reshape(1, WIDTH).astype(jnp.float16),
-                jnp.zeros((PACK_ROWS - TOK - 3, WIDTH), jnp.float16),
-            ],
-            axis=0,
+            7,
+        )(
+            history[0], req_rows[0, 0].T, req_counts[0], labels[0].T,
+            item_table, w_item_in, w_item_out,
         )
-        packed, embedding = lax.optimization_barrier((packed, embedding))
 
     with jax.named_scope("table_gather"):
         table = lax.all_gather(embedding, ("core", "item"), axis=0, tiled=True)
@@ -278,34 +310,23 @@
     with jax.named_scope("history_gather"):
         gathered = lax.all_gather(packed, ("z", "core"), axis=0, tiled=True)
 
-    with jax.named_scope("unpack"):
-        gathered = gathered.reshape(CHIPS, 2, PACK_ROWS, WIDTH)
-        histories = (gathered[:, :, :TOK].astype(F32) * (1.0 / CODE_SCALE)).astype(BF)
-        extras = lax.dynamic_slice(
-            gathered, (0, core, TOK, 0), (CHIPS, 1, 8, WIDTH)
-        ).reshape(CHIPS, 8, WIDTH).astype(F32)
-        label_rows = extras[:, 2]
-        asked = lax.dynamic_slice(extras[:, 0:2].reshape(CHIPS, 1024), (0, chip * 64), (CHIPS, 64))
-        asked = asked.reshape(CHIPS, 32, 2)
-        by_owner = asked.transpose(2, 0, 1).reshape(32, 32)
-        by_block = asked.transpose(2, 1, 0).reshape(64, CHIPS)
-        sender = core * 16 + lax.axis_index("item")
-        quarter = (jnp.arange(4) == sender % 4).astype(F32)
-        index = (by_owner.T[:, None, :] * quarter[None, :, None]).reshape(32, TOK)
-
     with jax.named_scope("tower"):
-        user_rows = call(
+        user_rows, asked_rows, label_rows = call(
             tower_kernel,
-            jax.ShapeDtypeStruct((HALF, WIDTH), BF),
+            (
+                jax.ShapeDtypeStruct((HALF, WIDTH), BF),
+                jax.ShapeDtypeStruct((32, TOK), F32),
+                jax.ShapeDtypeStruct((CHIPS, WIDTH), F32),
+            ),
             1,
             3,
             [
-                pltpu.VMEM((2 * HALF, HEADS * DQK), BF),
+                pltpu.VMEM((HEADS * DQK, 2 * HALF), BF),
                 pltpu.VMEM((2 * HALF, WIDTH), BF),
-                pltpu.VMEM((HEADS, 2 * TOK, 2 * DQK), BF),
-                pltpu.VMEM((2 * TOK, WIDTH), F32),
+                pltpu.VMEM((HEADS, TILE, 2 * DQK), BF),
+                pltpu.VMEM((TILE, WIDTH), F32),
             ],
-        )(place, histories, w_in, w_out)
+        )(place, gathered.reshape(CHIPS, 2, PACK_ROWS, WIDTH), w_in, w_out)
 
     with jax.named_scope("scores"):
         exps, hits, exchange = call(
@@ -316,9 +337,9 @@
                 jax.ShapeDtypeStruct((CHIPS, 24, TOK), F32),
             ),
             1,
-            5,
-            [pltpu.VMEM((4, 1024, 128), F32)],
-        )(place, table, user_rows, by_owner, by_block, label_rows)
+            4,
+            [pltpu.VMEM((5, 1024, 128), F32)],
+        )(place, table, user_rows, asked_rows, label_rows)
 
     with jax.named_scope("totals_exchange"):
         exchange = lax.all_to_all(exchange, "z", split_axis=0, concat_axis=0, tiled=True)
@@ -333,7 +354,7 @@
             1,
             6,
             [pltpu.VMEM((32 * SEND_ROWS, 128), F32)],
-        )(place, exps, hits, user_rows, exchange, label_rows, index)
+        )(place, exps, hits, user_rows, exchange, label_rows, asked_rows)
 
     with jax.named_scope("gradient_send"):
         arrived = lax.all_to_all(

time: 206 us -> 175 us (0.85)
  blocking collectives: 81.1 us -> 103 us
  Pallas kernels: 73.7 us -> 55.6 us
  waiting for transfers between devices: 12.2 us -> 0.02 us
  other arithmetic: 10.5 us -> 1.27 us
  local copies, waits for them, and re-layouts: 7.55 us -> 0.34 us
  starting transfers between devices: 6.52 us -> 0.04 us
    all_to_all x0 -> x1, blocking collectives: none -> 19.7 us  [on_device(): lax.all_to_all(exchange, 'z', split_axis=0, concat_axis=0, tiled=True)]
    pallas_call x2, Pallas kernels: 57.6 us -> 39.2 us  [the longest x1 36.1 us: on_device(): call(tower_kernel, (jax.ShapeDtypeStruct((HALF, WIDTH), BF), jax.ShapeDty...]
    all_to_all x1 -> x0, waiting for transfers between devices: 12.2 us -> none  [on_device(): lax.all_to_all(exchange, 'z', split_axis=0, concat_axis=0, tiled=True)]
    convert_element_type x5 -> x0, other arithmetic: 6.55 us -> none  [the longest x1 5.55 us: on_device(): (gathered[:, :, :TOK].astype(F32) * (1.0 / CODE_SCALE)).astype(BF)]
    all_to_all x1 -> x0, starting transfers between devices: 6.48 us -> none  [on_device(): lax.all_to_all(exchange, 'z', split_axis=0, concat_axis=0, tiled=True)]
    unnamed x12 -> x2, local copies, waits for them, and re-layouts: 4.39 us -> 0.33 us
    all_gather x1, blocking collectives: 52.6 us -> 55 us  [on_device(): gathered = lax.all_gather(packed, ('z', 'core'), axis=0, tiled=True)]
  transfers between devices with their start and end apart: 2 -> 1, of which waited for: 1 -> 0; matrix products, arithmetic and copies ran while one was open for 4% -> 0% of each run, Pallas kernels for 27% -> 21%
where the time goes in v2:
time: 175 us; the launch traced here: 174 us
  blocking collectives  103 us (59%)
  Pallas kernels  55.6 us (32%)
  between operations  14 us (8%)
    all_gather x1, blocking collectives, on_device(): gathered = lax.all_gather(packed, ('z', 'core'), axis=0, tiled=True)  55 us
    pallas_call x1, Pallas kernels, on_device(): call(tower_kernel, (jax.ShapeDtypeStruct((HALF, WIDTH), BF), jax.ShapeDty...  36.1 us
    all_to_all x1, blocking collectives, on_device(): lax.all_to_all(send.reshape(32, SEND_ROWS, 128), ('core', 'item'), split_...  28.3 us
    all_to_all x1, blocking collectives, on_device(): lax.all_to_all(exchange, 'z', split_axis=0, concat_axis=0, tiled=True)  19.7 us
    pallas_call x1, Pallas kernels, on_device(): call(scores_kernel, (jax.ShapeDtypeStruct((CHIPS, 64, TOK), F32), jax.Sha...  7.52 us
    pallas_call x1, Pallas kernels, on_device(): call(owner_kernel, jax.ShapeDtypeStruct((TOK, WIDTH), F32), 0, 6, [pltpu....  4.94 us
    pallas_call x1, Pallas kernels, on_device(): call(gradient_kernel, (jax.ShapeDtypeStruct((32 * SEND_ROWS, 128), BF), j...  3.93 us
  transfers between devices with their start and end apart: 1, of which 0 were waited for; matrix products, arithmetic and copies ran while one was open for 0% of the time, Pallas kernels for 21%

profile of v2, /device:TPU:1, one launch (start us, length us, event | category | flops | bytes accessed | tf_op | source)
XLA Modules:
  0.0 174.3 jit_solution(5952913893704584835)
XLA Ops:
  7.2 0.0 all-gather.3.cloned.1.call-start
  7.2 3.1 %prepare.1 = (s16[144,512]{1,0:T(8,128)(2,1)}, f32[128,1024]{1,0:T(8,128)}, f32[128,512]{1,0:T(8,128)}, bf16[128,512]{1,0:T(8,128)(2,1)}) custom-call(bf16[128,512]{1,0:T(8,128)(2,1)} %bitcast.20, s32[2,512]{1,0:T(2,128)} %bitcast.21, s32[1,512]{1,0:T(1,128)} %bitcast.22, s32[4,128]{1,0:T(4,128)} %bitcast.23, bf16[128,512]{1,0:T(8,128)(2,1)} %table_ref.1, ...), custom_call_target="tpu_custom_call" | custom-call | tf_op jit(solution)/shard_map/prepare/pallas_call | solution.py:292
  10.3 0.0 all-gather.3.cloned.1.call-update
  10.3 0.6 pad_add_fusion.place_ref
  10.9 55.0 %all-gather.4 = s16[4608,512]{1,0:T(8,128)(2,1)} all-gather(s16[144,512]{1,0:T(8,128)(2,1)} %get-tuple-element.15), channel_id=1, replica_groups=mesh['z'=16,'core'=2,'item'=16] {'z','core'}, dimensions={0}, use_global_device_ids=true | all-gather | bytes 4866048 | tf_op jit(solution)/shard_map/history_gather/all_gather | solution.py:311
  65.9 36.1 %tower.1 = (bf16[2048,512]{1,0:T(8,128)(2,1)}, f32[32,128]{1,0:T(8,128)}, f32[16,512]{1,0:T(8,128)}) custom-call(s32[3]{0:T(128)} %pad_add_fusion.place_ref, s16[16,2,144,512]{3,2,1,0:T(8,128)(2,1)} %bitcast.18, bf16[512,1536]{1,0:T(8,128)(2,1)} %w_in_ref.4, bf16[512,512]{1,0:T(8,128)(2,1)} %w_out_ref.4), custom_call_target="tpu_custom_call" | custom-call | tf_op jit(solution)/shard_map/tower/pallas_call | solution.py:314
  102.1 0.0 all-gather.3.cloned.1.call-done.table_ref
  102.1 7.5 %scores.1 = (f32[16,64,128]{2,1,0:T(8,128)}, f32[16,64,128]{2,1,0:T(8,128)}, f32[16,24,128]{2,1,0:T(8,128)}) custom-call(s32[3]{0:T(128)} %pad_add_fusion.place_ref, bf16[4096,512]{1,0:T(8,128)(2,1)} %all-gather.3.cloned.1.call-done.table_ref, bf16[2048,512]{1,0:T(8,128)(2,1)} %get-tuple-element.16.user_ref, f32[32,128]{1,0:T(8,128)} %get-tuple-element.17.rows_ref, ...), custom_call_target="tpu_custom_call" | custom-call | tf_op jit(solution)/shard_map/scores/pallas_call | solution.py:332
  109.6 19.7 %all_to_all.10.exchange_ref = f32[16,24,128]{2,1,0:T(8,128)} all-to-all(f32[16,24,128]{2,1,0:T(8,128)} %get-tuple-element.21), channel_id=1, replica_groups=mesh['z'=16,'core'=2,'item'=16] {'z'}, dimensions={0} | all-to-all | bytes 393216 | tf_op jit(solution)/shard_map/totals_exchange/all_to_all | solution.py:345
  129.3 3.9 %gradient_rows.1 = (bf16[4352,128]{1,0:T(8,128)(2,1)}, f32[1,128]{1,0:T(1,128)}) custom-call(s32[3]{0:T(128)} %pad_add_fusion.place_ref, f32[16,64,128]{2,1,0:T(8,128)} %get-tuple-element.19.exps_ref, f32[16,64,128]{2,1,0:T(8,128)} %get-tuple-element.20.hits_ref, bf16[2048,512]{1,0:T(8,128)(2,1)} %get-tuple-element.16.user_ref, ...), custom_call_target="tpu_custom_call" | custom-call | tf_op jit(solution)/shard_map/gradient_rows/pallas_call | solution.py:348
  133.2 28.3 %all_to_all.11.arrived_ref = bf16[32,136,128]{2,1,0:T(8,128)(2,1)S(1)} all-to-all(bf16[32,136,128]{2,1,0:T(8,128)(2,1)} %bitcast.19), channel_id=1, replica_groups=mesh['z'=16,'core'=2,'item'=16] {'core','item'}, dimensions={0} | all-to-all | bytes 2228224 | tf_op jit(solution)/shard_map/gradient_send/all_to_all | solution.py:360
  161.5 0.0 copy-start
  161.5 0.7 fusion.index_ref
  162.2 0.3 copy-done
  162.5 4.9 %owner.1 = f32[128,512]{1,0:T(8,128)} custom-call(bf16[32,136,128]{2,1,0:T(8,128)(2,1)} %copy-done, f32[32,128]{1,0:T(8,128)} %fusion.index_ref, f32[128,1024]{1,0:T(8,128)} %get-tuple-element.24.hidden_in_ref, f32[128,512]{1,0:T(8,128)} %get-tuple-element.25.raw_ref, bf16[512,1024]{1,0:T(8,128)(2,1)} %w_in_ref.5, bf16[1024,512]{1,0:T(8,128)(2,1)} %w_out_ref.5), custom_call_target="tpu_custom_call" | custom-call | tf_op jit(solution)/shard_map/owner/pallas_call | solution.py:365
  (1 shorter events, 0.0 us)
Async XLA Ops:
  7.2 94.9 %all-gather.3.cloned.1.call-start = ((), (), s32[]{:S(2)}) async-start(), calls=%async_computation.2 | async-start | bytes 4325376 | tf_op jit(solution)/shard_map/table_gather/all_gather | solution.py:308
  161.5 1.0 copy-start
Sparse Core Ops, SparseCore 0:
  11.2 67.0 all-gather.2

commit v3 on v2

--- a/solution.py
+++ b/solution.py
@@ -12,6 +12,7 @@
 WIDTH = 512
 HIDDEN = 1024
 CHIPS = 16
+ITEMS = 16
 HALF = CHIPS * TOK
 TILE = 512
 PACK_ROWS = 144
@@ -49,9 +50,8 @@
     return dot(high, weight, NT) + dot(low, weight, NT)
 
 
-def call(kernel, out_shape, n_smem, n_vmem, scratch=()):
-    space = [pl.BlockSpec(memory_space=pltpu.SMEM)] * n_smem
-    space += [pl.BlockSpec(memory_space=pltpu.VMEM)] * n_vmem
+def call(kernel, out_shape, inputs, scratch=()):
+    space = [pl.BlockSpec(memory_space=pltpu.VMEM)] * inputs
     return pl.pallas_call(
         kernel,
         out_shape=out_shape,
@@ -64,7 +64,7 @@
 
 def prepare_kernel(
     history_ref, wanted_ref, counts_ref, labels_ref, table_ref, w_in_ref, w_out_ref,
-    packed_ref, hidden_in_ref, raw_ref, embedding_ref,
+    packed_ref, hidden_in_ref, raw_ref, copies_ref,
 ):
     rows = history_ref[...].astype(F32)
     root = jnp.exp(jnp.log(jnp.abs(rows) * (1.0 / RANGE)) * (1.0 / 3.0)) * CODES
@@ -83,7 +83,9 @@
     raw = dot(silu(hidden_in).astype(BF), w_out_ref[...])
     raw_ref[...] = raw
     inv_norm = lax.rsqrt(jnp.sum(raw * raw, axis=-1, keepdims=True) + unit_eps)
-    embedding_ref[...] = (raw * inv_norm).astype(BF)
+    embedding = (raw * inv_norm).astype(BF)
+    for rank in range(ITEMS):
+        copies_ref[rank] = embedding
 
 
 def decode(codes):
@@ -92,15 +94,18 @@
 
 
 def tower_kernel(
-    place_ref, packed_ref, w_in_ref, w_out_ref, user_ref, rows_ref, labels_ref,
+    packed_ref, w_in_ref, w_out_ref, user_ref, rows_ref, labels_ref,
     key_scr, value_scr, query_scr, total_scr,
 ):
-    parity = place_ref[0]
-    chip = place_ref[1]
-
+    parity = lax.axis_index("core")
+    chip = lax.axis_index("z")
+
+    first = lax.broadcasted_iota(jnp.int32, (16, WIDTH), 1) < ITEMS
+    near = WIDTH - chip * 32 - parity * ITEMS
+    far = lax.rem(WIDTH + ITEMS - chip * 32 - (1 - parity) * ITEMS, WIDTH)
     for block in range(CHIPS):
         extras = packed_ref[block, parity, TOK:PACK_ROWS, :].astype(F32)
-        mine = pltpu.roll(extras, WIDTH - chip * 32, 1)
+        mine = jnp.where(first, pltpu.roll(extras, near, 1), pltpu.roll(extras, far, 1))
         rows_ref[block : block + 1, :] = mine[0:1, 0:TOK]
         rows_ref[CHIPS + block : CHIPS + block + 1, :] = mine[1:2, 0:TOK]
         labels_ref[block : block + 1, :] = extras[2:3]
@@ -172,22 +177,24 @@
         user_ref[group * TILE : (group + 1) * TILE, :] = (updated * scale).astype(BF)
 
 
-def label_places(labels_ref, block, entry, chip):
+def label_places(labels_ref, block, entry, chip, core):
     label = labels_ref[block : block + 1, entry * TOK : (entry + 1) * TOK].astype(jnp.int32)
     local = label - chip * 64
     inside = (label >= 0) & (local >= 0) & (local < 64)
-    return jnp.where(inside, (local & 1) * 32 + (local >> 1), -1)
+    return jnp.where(inside, (local & 1) * 32 + ((local >> 1) ^ (core * ITEMS)), -1)
 
 
 def scores_kernel(
-    place_ref, table_ref, user_ref, rows_ref, labels_ref,
+    near_ref, far_ref, user_ref, rows_ref, labels_ref,
     exps_ref, hits_ref, exchange_ref, entry_scr,
 ):
-    chip = place_ref[1]
+    chip = lax.axis_index("z")
+    core = lax.axis_index("core")
     row_ids = lax.broadcasted_iota(jnp.int32, (32, TOK), 1).astype(F32)
     for owner in range(32):
         asked = jnp.broadcast_to(rows_ref[:, owner : owner + 1], (32, TOK))
-        rows = dot((row_ids == asked).astype(BF), table_ref[owner * TOK : (owner + 1) * TOK, :])
+        table = (far_ref if owner // ITEMS else near_ref)[owner % ITEMS]
+        rows = dot((row_ids == asked).astype(BF), table)
         used = (asked >= 0.0).astype(F32)
         for slot in range(2):
             entry_scr[4, pl.ds(slot * 32 + owner, 16, stride=64), :] = used[
@@ -209,7 +216,7 @@
         exps_ref[block] = exps
         hits = jnp.zeros((64, TOK), F32)
         for entry in range(4):
-            place = label_places(labels_ref, block, entry, chip)
+            place = label_places(labels_ref, block, entry, chip, core)
             hits = hits + (slot_ids == place).astype(F32)
         hits_ref[block] = hits
         total = jnp.sum(exps, axis=0, keepdims=True)
@@ -218,10 +225,11 @@
 
 
 def gradient_kernel(
-    place_ref, exps_ref, hits_ref, user_ref, exchange_ref, labels_ref, rows_ref,
-    send_ref, loss_ref, grad_scr,
-):
-    chip = place_ref[1]
+    exps_ref, hits_ref, user_ref, exchange_ref, labels_ref, rows_ref,
+    near_ref, far_ref, loss_ref, near_scr, far_scr,
+):
+    chip = lax.axis_index("z")
+    sides = (near_scr, far_scr)
     sums = jnp.sum(exchange_ref[...], axis=0)
     positives = jnp.zeros((CHIPS, TOK), F32)
     for entry in range(4):
@@ -241,34 +249,43 @@
         grads = dot(score_grad, user_ref[block * TOK : (block + 1) * TOK, :]) * inverse_sharpness
         for slot in range(2):
             for part in range(4):
-                at = part * 32 + slot * 16 + block
-                grad_scr[pl.ds(at, 32, stride=SEND_ROWS), :] = grads[
-                    slot * 32 : (slot + 1) * 32, part * 128 : (part + 1) * 128
-                ]
-    at = lax.broadcasted_iota(jnp.int32, (32, TOK), 0) + (place_ref[2] & 3) * 32
+                for side in range(2):
+                    at = part * 32 + slot * 16 + block
+                    first = slot * 32 + side * 16
+                    sides[side][pl.ds(at, 16, stride=SEND_ROWS), :] = grads[
+                        first : first + 16, part * 128 : (part + 1) * 128
+                    ]
+    at = lax.broadcasted_iota(jnp.int32, (32, TOK), 0) + (lax.axis_index("item") & 3) * 32
     spread = (lax.broadcasted_iota(jnp.int32, (32, TOK), 1) == at).astype(BF)
     index = dot(rows_ref[...].astype(BF), spread, (((0,), (0,)), ((), ())))[0:32]
-    zeros = jnp.zeros((32, TOK), F32)
-    for extra in range(8):
-        grad_scr[pl.ds(TOK + extra, 32, stride=SEND_ROWS), :] = zeros if extra else index
-    send_ref[...] = grad_scr[...].astype(BF)
+    zeros = jnp.zeros((16, TOK), F32)
+    for side in range(2):
+        for extra in range(8):
+            rows = zeros if extra else index[side * 16 : (side + 1) * 16]
+            sides[side][pl.ds(TOK + extra, 16, stride=SEND_ROWS), :] = rows
+    near_ref[...] = near_scr[...].astype(BF)
+    far_ref[...] = far_scr[...].astype(BF)
 
 
 def owner_kernel(
-    arrived_ref, index_ref, hidden_in_ref, raw_ref, w_in_ref, w_out_ref, gradient_ref, rows_scr
+    arrived_ref, hidden_in_ref, raw_ref, w_in_ref, w_out_ref, gradient_ref, rows_scr
 ):
     row_ids = lax.broadcasted_iota(jnp.int32, (TOK, TOK), 0).astype(F32)
     row_grad = jnp.zeros((TOK, WIDTH), F32)
-    for group in range(8):
-        index = jnp.zeros((1, TOK), F32)
+    for group in range(4):
+        extras = jnp.zeros((16, TOK), F32)
         for member in range(4):
             sender = group * 4 + member
-            index = index + index_ref[sender : sender + 1, :]
-            for part in range(4):
-                rows_scr[member * 32 : (member + 1) * 32, part * 128 : (part + 1) * 128] = arrived_ref[
-                    sender, part * 32 : (part + 1) * 32, :
-                ]
-        pick = (row_ids == index).astype(BF)
+            extras = extras + arrived_ref[sender, 2 * TOK :, :].astype(F32)
+            for side in range(2):
+                for part in range(4):
+                    first = side * TOK + part * 32
+                    rows_scr[
+                        side * TOK + member * 32 : side * TOK + (member + 1) * 32,
+                        part * 128 : (part + 1) * 128,
+                    ] = arrived_ref[sender, first : first + 32, :]
+        index = jnp.concatenate([extras[0:1], extras[8:9]], axis=1)
+        pick = (jnp.concatenate([row_ids, row_ids], axis=1) == index).astype(BF)
         row_grad = row_grad + dot(pick, rows_scr[...])
     raw = raw_ref[...]
     inv_norm = lax.rsqrt(jnp.sum(raw * raw, axis=-1, keepdims=True) + unit_eps)
@@ -284,20 +301,17 @@
 def on_device(
     history, w_in, w_out, item_table, w_item_in, w_item_out, req_rows, req_counts, labels
 ):
-    chip = lax.axis_index("z")
-    core = lax.axis_index("core")
-    place = jnp.stack([core, chip, lax.axis_index("item")]).astype(jnp.int32)
+    swap = [(0, 1), (1, 0)]
 
     with jax.named_scope("prepare"):
-        packed, hidden_in, raw_embed, embedding = call(
+        packed, hidden_in, raw_embed, copies = call(
             prepare_kernel,
             (
                 jax.ShapeDtypeStruct((PACK_ROWS, WIDTH), jnp.int16),
                 jax.ShapeDtypeStruct((TOK, HIDDEN), F32),
                 jax.ShapeDtypeStruct((TOK, WIDTH), F32),
-                jax.ShapeDtypeStruct((TOK, WIDTH), BF),
+                jax.ShapeDtypeStruct((ITEMS, TOK, WIDTH), BF),
             ),
-            0,
             7,
         )(
             history[0], req_rows[0, 0].T, req_counts[0], labels[0].T,
@@ -305,10 +319,14 @@
         )
 
     with jax.named_scope("table_gather"):
-        table = lax.all_gather(embedding, ("core", "item"), axis=0, tiled=True)
+        near_table = lax.all_to_all(copies, "item", split_axis=0, concat_axis=0, tiled=True)
 
     with jax.named_scope("history_gather"):
         gathered = lax.all_gather(packed, ("z", "core"), axis=0, tiled=True)
+        gathered, near_table = lax.optimization_barrier((gathered, near_table))
+
+    with jax.named_scope("table_swap"):
+        far_table = lax.ppermute(near_table, "core", swap)
 
     with jax.named_scope("tower"):
         user_rows, asked_rows, label_rows = call(
@@ -318,7 +336,6 @@
                 jax.ShapeDtypeStruct((32, TOK), F32),
                 jax.ShapeDtypeStruct((CHIPS, WIDTH), F32),
             ),
-            1,
             3,
             [
                 pltpu.VMEM((HEADS * DQK, 2 * HALF), BF),
@@ -326,7 +343,7 @@
                 pltpu.VMEM((HEADS, TILE, 2 * DQK), BF),
                 pltpu.VMEM((TILE, WIDTH), F32),
             ],
-        )(place, gathered.reshape(CHIPS, 2, PACK_ROWS, WIDTH), w_in, w_out)
+        )(gathered.reshape(CHIPS, 2, PACK_ROWS, WIDTH), w_in, w_out)
 
     with jax.named_scope("scores"):
         exps, hits, exchange = call(
@@ -336,39 +353,40 @@
                 jax.ShapeDtypeStruct((CHIPS, 64, TOK), F32),
                 jax.ShapeDtypeStruct((CHIPS, 24, TOK), F32),
             ),
-            1,
-            4,
+            5,
             [pltpu.VMEM((5, 1024, 128), F32)],
-        )(place, table, user_rows, asked_rows, label_rows)
+        )(near_table, far_table, user_rows, asked_rows, label_rows)
 
     with jax.named_scope("totals_exchange"):
         exchange = lax.all_to_all(exchange, "z", split_axis=0, concat_axis=0, tiled=True)
 
     with jax.named_scope("gradient_rows"):
-        send, loss = call(
+        near, far, loss = call(
             gradient_kernel,
             (
-                jax.ShapeDtypeStruct((32 * SEND_ROWS, 128), BF),
+                jax.ShapeDtypeStruct((ITEMS * SEND_ROWS, 128), BF),
+                jax.ShapeDtypeStruct((ITEMS * SEND_ROWS, 128), BF),
                 jax.ShapeDtypeStruct((1, TOK), F32),
             ),
-            1,
             6,
-            [pltpu.VMEM((32 * SEND_ROWS, 128), F32)],
-        )(place, exps, hits, user_rows, exchange, label_rows, asked_rows)
+            [pltpu.VMEM((ITEMS * SEND_ROWS, 128), F32)] * 2,
+        )(exps, hits, user_rows, exchange, label_rows, asked_rows)
+
+    with jax.named_scope("gradient_swap"):
+        near = near.reshape(ITEMS, SEND_ROWS, 128)
+        far = lax.ppermute(far.reshape(ITEMS, SEND_ROWS, 128), "core", swap)
+        send = jnp.concatenate([near[:, :TOK], far[:, :TOK], near[:, TOK:], far[:, TOK:]], axis=1)
 
     with jax.named_scope("gradient_send"):
-        arrived = lax.all_to_all(
-            send.reshape(32, SEND_ROWS, 128), ("core", "item"), split_axis=0, concat_axis=0, tiled=True
-        )
+        arrived = lax.all_to_all(send, "item", split_axis=0, concat_axis=0, tiled=True)
 
     with jax.named_scope("owner"):
         gradient = call(
             owner_kernel,
             jax.ShapeDtypeStruct((TOK, WIDTH), F32),
-            0,
-            6,
-            [pltpu.VMEM((TOK, WIDTH), BF)],
-        )(arrived, arrived[:, TOK].astype(F32), hidden_in, raw_embed, w_item_in, w_item_out)
+            5,
+            [pltpu.VMEM((2 * TOK, WIDTH), BF)],
+        )(arrived, hidden_in, raw_embed, w_item_in, w_item_out)
     return (loss, gradient)
 
 

time: 175 us -> 174 us (level)
  starting transfers between devices: 0.04 us -> 15 us
  between operations: 14 us -> 0.72 us
  blocking collectives: 103 us -> 97.5 us
  local copies, waits for them, and re-layouts: 0.34 us -> 3.22 us
    all_to_all x0 -> x1, starting transfers between devices: none -> 7.72 us  [on_device(): lax.all_to_all(copies, 'item', split_axis=0, concat_axis=0, tiled=True)]
    ppermute x0 -> x2, starting transfers between devices: none -> 7.29 us  [the longest x1 5.24 us: on_device(): far = lax.ppermute(far.reshape(ITEMS, SEND_ROWS, 128), 'core', swap)]
    all_to_all x1, blocking collectives: 28.3 us -> 24.3 us  [on_device(): lax.all_to_all(send, 'item', split_axis=0, concat_axis=0, tiled=True)]
    slice x1 -> x4, local copies, waits for them, and re-layouts: 0.01 us -> 1.89 us  [the longest x1 1.08 us: on_device(): near[:, :TOK]]
  transfers between devices with their start and end apart: 1 -> 3, of which waited for: 0 -> 0; matrix products, arithmetic and copies ran while one was open for 0% -> 1% of each run, Pallas kernels for 21% -> 21%
where the time goes in v3:
time: 174 us; the launch traced here: 173 us
  blocking collectives  97.5 us (56%)
  Pallas kernels  56.2 us (32%)
  starting transfers between devices  15 us (9%)
  local copies, waits for them, and re-layouts  3.22 us (2%)
    all_gather x1, blocking collectives, on_device(): gathered = lax.all_gather(packed, ('z', 'core'), axis=0, tiled=True)  53.6 us
    pallas_call x1, Pallas kernels, on_device(): call(tower_kernel, (jax.ShapeDtypeStruct((HALF, WIDTH), BF), jax.ShapeDty...  36 us
    all_to_all x1, blocking collectives, on_device(): lax.all_to_all(send, 'item', split_axis=0, concat_axis=0, tiled=True)  24.3 us
    all_to_all x1, blocking collectives, on_device(): lax.all_to_all(exchange, 'z', split_axis=0, concat_axis=0, tiled=True)  19.6 us
    all_to_all x1, starting transfers between devices, on_device(): lax.all_to_all(copies, 'item', split_axis=0, concat_axis=0, tiled=True)  7.72 us
    pallas_call x1, Pallas kernels, on_device(): call(scores_kernel, (jax.ShapeDtypeStruct((CHIPS, 64, TOK), F32), jax.Sha...  7.62 us
    ppermute x1, starting transfers between devices, on_device(): far = lax.ppermute(far.reshape(ITEMS, SEND_ROWS, 128), 'core', swap)  5.24 us
    pallas_call x1, Pallas kernels, on_device(): call(owner_kernel, jax.ShapeDtypeStruct((TOK, WIDTH), F32), 5, [pltpu.VME...  4.87 us
  transfers between devices with their start and end apart: 3, of which 0 were waited for; matrix products, arithmetic and copies ran while one was open for 1% of the time, Pallas kernels for 21%

profile of v3, /device:TPU:1, one launch (start us, length us, event | category | flops | bytes accessed | tf_op | source)
XLA Modules:
  0.0 172.7 jit_solution(3077926240565545804)
XLA Ops:
  0.6 3.8 %prepare.1 = (s16[144,512]{1,0:T(8,128)(2,1)}, f32[128,1024]{1,0:T(8,128)}, f32[128,512]{1,0:T(8,128)}, bf16[16,128,512]{2,1,0:T(8,128)(2,1)}) custom-call(bf16[128,512]{1,0:T(8,128)(2,1)} %bitcast.14, s32[2,512]{1,0:T(2,128)} %bitcast.15, s32[1,512]{1,0:T(1,128)} %bitcast.16, s32[4,128]{1,0:T(4,128)} %bitcast.17, bf16[128,512]{1,0:T(8,128)(2,1)} %table_ref.1, ...), custom_call_target="tpu_custom_call" | custom-call | tf_op jit(solution)/shard_map/prepare/pallas_call | solution.py:307
  4.4 0.0 copy-start.2
  4.4 7.7 %all-to-all-start = ((bf16[16,128,512]{2,1,0:T(8,128)(2,1)}), bf16[16,128,512]{2,1,0:T(8,128)(2,1)S(1)}, u32[]{:S(2)}, u32[]{:S(2)}) async-start(bf16[16,128,512]{2,1,0:T(8,128)(2,1)} %get-tuple-element.18), calls=%async_computation | async-start | bytes 4194304 | tf_op jit(solution)/shard_map/table_gather/all_to_all | solution.py:322
  12.2 0.0 copy-done.2
  12.2 53.6 %all-gather.1 = s16[4608,512]{1,0:T(8,128)(2,1)} all-gather(s16[144,512]{1,0:T(8,128)(2,1)S(1)} %copy-done.2), channel_id=1, replica_groups=mesh['z'=16,'core'=2,'item'=16] {'z','core'}, dimensions={0}, use_global_device_ids=true | all-gather | bytes 4866048 | tf_op jit(solution)/shard_map/history_gather/all_gather | solution.py:325
  65.8 0.0 all-to-all-done.near_ref
  65.8 0.0 copy-start
  65.8 2.0 %collective-permute-start = (bf16[16,128,512]{2,1,0:T(8,128)(2,1)S(1)}, bf16[16,128,512]{2,1,0:T(8,128)(2,1)S(1)}, u32[]{:S(2)}, u32[]{:S(2)}) collective-permute-start(bf16[16,128,512]{2,1,0:T(8,128)(2,1)S(1)} %all-to-all-done.near_ref), channel_id=1, source_target_pairs={{0,16},{16,0},{1,17},{17,1},{2,18},{18,2},{3,19},{19,3},{4,20},{20... | collective-permute-start | bytes 6291464 | tf_op jit(solution)/shard_map/table_swap/ppermute | solution.py:329
  67.8 36.0 %tower.1 = (bf16[2048,512]{1,0:T(8,128)(2,1)}, f32[32,128]{1,0:T(8,128)}, f32[16,512]{1,0:T(8,128)}) custom-call(s16[16,2,144,512]{3,2,1,0:T(8,128)(2,1)} %bitcast.11, bf16[512,1536]{1,0:T(8,128)(2,1)} %w_in_ref.4, bf16[512,512]{1,0:T(8,128)(2,1)} %w_out_ref.4), custom_call_target="tpu_custom_call" | custom-call | tf_op jit(solution)/shard_map/tower/pallas_call | solution.py:332
  103.8 0.0 copy-done
  103.8 0.0 collective-permute-done.far_ref
  103.8 0.0 copy-start.1
  103.9 1.3 copy-done.1
  105.2 7.6 %scores.1 = (f32[16,64,128]{2,1,0:T(8,128)}, f32[16,64,128]{2,1,0:T(8,128)}, f32[16,24,128]{2,1,0:T(8,128)}) custom-call(bf16[16,128,512]{2,1,0:T(8,128)(2,1)} %copy-done, bf16[16,128,512]{2,1,0:T(8,128)(2,1)} %copy-done.1, bf16[2048,512]{1,0:T(8,128)(2,1)} %get-tuple-element.21.user_ref, f32[32,128]{1,0:T(8,128)} %get-tuple-element.22.rows_ref, ...), custom_call_target="tpu_custom_call" | custom-call | tf_op jit(solution)/shard_map/scores/pallas_call | solution.py:349
  112.8 19.6 %all_to_all.15.exchange_ref = f32[16,24,128]{2,1,0:T(8,128)} all-to-all(f32[16,24,128]{2,1,0:T(8,128)} %get-tuple-element.26), channel_id=1, replica_groups=mesh['z'=16,'core'=2,'item'=16] {'z'}, dimensions={0} | all-to-all | bytes 393216 | tf_op jit(solution)/shard_map/totals_exchange/all_to_all | solution.py:361
  132.4 3.9 %gradient_rows.1 = (bf16[2176,128]{1,0:T(8,128)(2,1)}, bf16[2176,128]{1,0:T(8,128)(2,1)}, f32[1,128]{1,0:T(1,128)}) custom-call(f32[16,64,128]{2,1,0:T(8,128)} %get-tuple-element.24.exps_ref, f32[16,64,128]{2,1,0:T(8,128)} %get-tuple-element.25.hits_ref, bf16[2048,512]{1,0:T(8,128)(2,1)} %get-tuple-element.21.user_ref, ...), custom_call_target="tpu_custom_call" | custom-call | tf_op jit(solution)/shard_map/gradient_rows/pallas_call | solution.py:364
  136.3 5.2 %collective-permute-start.1 = (bf16[16,136,128]{2,1,0:T(8,128)(2,1)}, bf16[16,136,128]{2,1,0:T(8,128)(2,1)S(1)}, u32[]{:S(2)}, u32[]{:S(2)}) collective-permute-start(bf16[16,136,128]{2,1,0:T(8,128)(2,1)} %bitcast.18), channel_id=1, source_target_pairs={{0,16},{16,0},{1,17},{17,1},{2,18},{18,2},{3,19},{19,3},{4,20},{20... | collective-permute-start | bytes 1671176 | tf_op jit(solution)/shard_map/gradient_swap/ppermute | solution.py:377
  141.5 0.8 slice.18
  142.3 1.1 slice.16
  143.4 0.0 collective-permute-done.1
  143.5 0.1 pad_maximum_fusion
  143.6 24.3 %all_to_all.16.arrived_ref = bf16[16,272,128]{2,1,0:T(8,128)(2,1)} all-to-all(bf16[16,272,128]{2,1,0:T(8,128)(2,1)S(1)} %pad_maximum_fusion), channel_id=1, replica_groups=mesh['z'=16,'core'=2,'item'=16] {'item'}, dimensions={0} | all-to-all | bytes 2228224 | tf_op jit(solution)/shard_map/gradient_send/all_to_all | solution.py:381
  167.8 4.9 %owner.1 = f32[128,512]{1,0:T(8,128)} custom-call(bf16[16,272,128]{2,1,0:T(8,128)(2,1)} %all_to_all.16.arrived_ref, f32[128,1024]{1,0:T(8,128)} %get-tuple-element.30.hidden_in_ref, f32[128,512]{1,0:T(8,128)} %get-tuple-element.31.raw_ref, bf16[512,1024]{1,0:T(8,128)(2,1)} %w_in_ref.5, bf16[1024,512]{1,0:T(8,128)(2,1)} %w_out_ref.5), custom_call_target="tpu_custom_call" | custom-call | tf_op jit(solution)/shard_map/owner/pallas_call | solution.py:384
  (2 shorter events, 0.1 us)
Async XLA Ops:
  4.4 7.7 %copy-start.2 = (s16[144,512]{1,0:T(8,128)(2,1)S(1)}, s16[144,512]{1,0:T(8,128)(2,1)}, u32[]{:S(2)}) copy-start(s16[144,512]{1,0:T(8,128)(2,1)} %get-tuple-element.17) | copy-start | bytes 442372
  4.4 61.4 %all-to-all-start = ((bf16[16,128,512]{2,1,0:T(8,128)(2,1)}), bf16[16,128,512]{2,1,0:T(8,128)(2,1)S(1)}, u32[]{:S(2)}, u32[]{:S(2)}) async-start(bf16[16,128,512]{2,1,0:T(8,128)(2,1)} %get-tuple-element.18), calls=%async_computation | async-start | bytes 4194304 | tf_op jit(solution)/shard_map/table_gather/all_to_all | solution.py:322
  65.8 38.1 %copy-start = (bf16[16,128,512]{2,1,0:T(8,128)(2,1)}, bf16[16,128,512]{2,1,0:T(8,128)(2,1)S(1)}, u32[]{:S(2)}) copy-start(bf16[16,128,512]{2,1,0:T(8,128)(2,1)S(1)} %all-to-all-done.near_ref) | copy-start | bytes 6291460
  65.8 38.1 %collective-permute-start = (bf16[16,128,512]{2,1,0:T(8,128)(2,1)S(1)}, bf16[16,128,512]{2,1,0:T(8,128)(2,1)S(1)}, u32[]{:S(2)}, u32[]{:S(2)}) collective-permute-start(bf16[16,128,512]{2,1,0:T(8,128)(2,1)S(1)} %all-to-all-done.near_ref), channel_id=1, source_target_pairs={{0,16},{16,0},{1,17},{17,1},{2,18},{18,2},{3,19},{19,3},{4,20},{20... | collective-permute-start | bytes 6291464 | tf_op jit(solution)/shard_map/table_swap/ppermute | solution.py:329
  103.8 1.3 copy-start.1
  136.3 7.1 %collective-permute-start.1 = (bf16[16,136,128]{2,1,0:T(8,128)(2,1)}, bf16[16,136,128]{2,1,0:T(8,128)(2,1)S(1)}, u32[]{:S(2)}, u32[]{:S(2)}) collective-permute-start(bf16[16,136,128]{2,1,0:T(8,128)(2,1)} %bitcast.18), channel_id=1, source_target_pairs={{0,16},{16,0},{1,17},{17,1},{2,18},{18,2},{3,19},{19,3},{4,20},{20... | collective-permute-start | bytes 1671176 | tf_op jit(solution)/shard_map/gradient_swap/ppermute | solution.py:377
